TPU v7x, 32 devices: a whole 2x2x4 slice. The times are simulated.
32 devices in a mesh: fsdp: 2 (over x), rows: 16 (over z, y, core).
Axes of the slice: x: 2, y: 2, z: 4, core: 2. Of those that a mesh axis runs over, the one named last changes fastest.
Arguments:
- residual_target: float32 [2, 12, 128, 512], P('fsdp', None, 'rows'), may hold values from -40 to 40
- conditioning: float32 [2, 12, 128, 512], P('fsdp', None, 'rows'), may hold values from -20 to 20
- noise_sample: float32 [2, 12, 128, 512], P('fsdp', None, 'rows'), may hold values from -20 to 20
- noise_level: int32 [2], P('fsdp'), may hold values from 0 to 63
- input_kernel: float32 [9, 64, 24], P(None, 'fsdp'), may hold values from -0.4375 to 0.4375
- first_kernel: float32 [9, 64, 64], P(None, 'fsdp'), may hold values from -0.25 to 0.25
- second_kernel: float32 [9, 64, 64], P(None, 'fsdp'), may hold values from -0.25 to 0.25
- down_kernel: float32 [9, 128, 64], P(None, 'fsdp'), may hold values from -0.25 to 0.25
- coarse_kernel: float32 [9, 128, 128], P(None, 'fsdp'), may hold values from -0.1875 to 0.1875
- upward_kernel: float32 [9, 64, 128], P(None, 'fsdp'), may hold values from -0.1875 to 0.1875
- output_kernel: float32 [9, 12, 64], P(None, None, 'fsdp'), may hold values from -0.25 to 0.25
- embed_matrix: float32 [128, 64], P('fsdp'), may hold values from -0.5 to 0.5
Outputs:
- denoised: float32 [2, 12, 128, 512], P('fsdp', None, 'rows')
- loss_value: float32 [], replicated
- input_grad: float32 [9, 64, 24], P(None, 'fsdp')
- first_grad: float32 [9, 64, 64], P(None, 'fsdp')
- second_grad: float32 [9, 64, 64], P(None, 'fsdp')
- down_grad: float32 [9, 128, 64], P(None, 'fsdp')
- coarse_grad: float32 [9, 128, 128], P(None, 'fsdp')
- upward_grad: float32 [9, 64, 128], P(None, 'fsdp')
- output_grad: float32 [9, 12, 64], P(None, None, 'fsdp')
- embed_grad: float32 [128, 64], P('fsdp')
All inputs are finite; a program needn't handle non-finite values.
Results may differ from a plain program's by a relative error of at most 0.03.
Values may be sent and summed in bfloat16 or wider, within the bound.
No kernel may reach another device: no remote copies, remote signals or barrier semaphores. Data moves between devices by JAX's collectives and lax.ppermute only.
A program may use at most 128 MiB of HBM per device.

v0:
```python
import jax
import jax.numpy as jnp
from jax import lax
from jax.sharding import PartitionSpec as P

GROUPS = 32
STEPS = 64


sigma_low = 0.002
sigma_high = 80.0
sigma_data = 0.5
rho_power = 7.0
eps_norm = 1e-05


def padded_2(block, sides, width):
    for axis, dim in sides:
        count = lax.axis_size(axis)
        forward = [(i, i + 1) for i in range(count - 1)]
        backward = [(target, source) for source, target in forward]
        low = lax.ppermute(
            lax.slice_in_dim(block, block.shape[dim] - width, None, axis=dim), axis, forward
        )
        high = lax.ppermute(lax.slice_in_dim(block, 0, width, axis=dim), axis, backward)
        block = jnp.concatenate([low, block, high], axis=dim)
    return block


def preconditions(level_index):
    ramp_value = level_index.astype(jnp.float32) / (STEPS - 1)
    top_root = sigma_high ** (1.0 / rho_power)
    bottom = sigma_low ** (1.0 / rho_power)
    sigma_level = (top_root + ramp_value * (bottom - top_root)) ** rho_power
    sigma_total = sigma_level * sigma_level + sigma_data * sigma_data
    skip_scale = sigma_data * sigma_data / sigma_total
    out_scale = sigma_level * sigma_data * lax.rsqrt(sigma_total)
    in_scale = lax.rsqrt(sigma_total)
    weight = sigma_total / (sigma_level * sigma_data) ** 2
    return (sigma_level, skip_scale, out_scale, in_scale, weight)


def embedding(sigma_level, features):
    half_count = features // 2
    ramp_steps = jnp.arange(half_count, dtype=jnp.float32) / half_count
    frequency = 64.0 * 0.01**ramp_steps
    phase_angle = 0.25 * jnp.log(sigma_level) * frequency
    return jnp.concatenate([jnp.cos(phase_angle), jnp.sin(phase_angle)]).astype(jnp.bfloat16)


def tap_products(padded, kernels, height, breadth):
    summed = jnp.zeros((kernels.shape[1], height, breadth), jnp.float32)
    for position in range(9):
        row_shift = position // 3
        col_shift = position % 3
        window = padded[:, row_shift : row_shift + height, col_shift : col_shift + breadth]
        summed = summed + jnp.einsum(
            "oc,chw->ohw", kernels[position], window, preferred_element_type=jnp.float32
        )
    return summed


def kernel_grad(padded, upstream):
    height, breadth = (upstream.shape[1], upstream.shape[2])
    parts = []
    for position in range(9):
        row_shift = position // 3
        col_shift = position % 3
        window = padded[:, row_shift : row_shift + height, col_shift : col_shift + breadth]
        parts.append(
            jnp.einsum("ohw,chw->oc", upstream, window, preferred_element_type=jnp.float32)
        )
    return jnp.stack(parts)


def band_convolve(source, kernels):
    rimmed = padded_2(source, (("rows", 1),), 1)
    padded = jnp.pad(rimmed, ((0, 0), (0, 0), (1, 1)))
    return (tap_products(padded, kernels, source.shape[1], source.shape[2]), padded)


def transposed(kernels):
    return jnp.transpose(kernels[::-1], (0, 2, 1))


def norm_forward(values, groups):
    channels, height, breadth = values.shape
    grouped = values.reshape(groups, channels // groups, height, breadth)
    total_sum, squares = lax.psum(
        (jnp.sum(grouped, axis=(1, 2, 3)), jnp.sum(grouped * grouped, axis=(1, 2, 3))), "rows"
    )
    members = channels // groups * height * breadth * lax.axis_size("rows")
    group_mean = total_sum / members
    inverse = lax.rsqrt(squares / members - group_mean * group_mean + eps_norm)
    normed = (grouped - group_mean[:, None, None, None]) * inverse[:, None, None, None]
    return (normed.reshape(values.shape), inverse)


def activate(normed):
    return jax.nn.silu(normed).astype(jnp.bfloat16)


def norm_backward(upstream, normed, inverse, groups):
    channels, height, breadth = normed.shape
    sigmoid = jax.nn.sigmoid(normed)
    grad_hat = (upstream * sigmoid * (1.0 + normed * (1.0 - sigmoid))).reshape(
        groups, channels // groups, height, breadth
    )
    hat_grouped = normed.reshape(groups, channels // groups, height, breadth)
    grad_total, cross_total = lax.psum(
        (jnp.sum(grad_hat, axis=(1, 2, 3)), jnp.sum(grad_hat * hat_grouped, axis=(1, 2, 3))), "rows"
    )
    members = channels // groups * height * breadth * lax.axis_size("rows")
    grad_mean = grad_total / members
    cross_mean = cross_total / members
    result = inverse[:, None, None, None] * (
        grad_hat - grad_mean[:, None, None, None] - hat_grouped * cross_mean[:, None, None, None]
    )
    return result.reshape(normed.shape)


def pool_down(values):
    channels, height, breadth = values.shape
    return 0.25 * values.reshape(channels, height // 2, 2, breadth // 2, 2).sum(axis=(2, 4))


def lift_up(values):
    return jnp.repeat(jnp.repeat(values, 2, axis=1), 2, axis=2)


def lift_back(values):
    channels, height, breadth = values.shape
    return values.reshape(channels, height // 2, 2, breadth // 2, 2).sum(axis=(2, 4))


def per_device(
    residual_target,
    conditioning,
    noise_sample,
    noise_level,
    input_kernel,
    first_kernel,
    second_kernel,
    down_kernel,
    coarse_kernel,
    upward_kernel,
    output_kernel,
    embed_matrix,
):
    (
        input_taps,
        first_taps,
        second_taps,
        down_taps,
        coarse_taps,
        upward_taps,
        output_taps,
        embed_taps,
    ) = (
        lax.all_gather(input_kernel.astype(jnp.bfloat16), "fsdp", axis=1, tiled=True),
        lax.all_gather(first_kernel.astype(jnp.bfloat16), "fsdp", axis=1, tiled=True),
        lax.all_gather(second_kernel.astype(jnp.bfloat16), "fsdp", axis=1, tiled=True),
        lax.all_gather(down_kernel.astype(jnp.bfloat16), "fsdp", axis=1, tiled=True),
        lax.all_gather(coarse_kernel.astype(jnp.bfloat16), "fsdp", axis=1, tiled=True),
        lax.all_gather(upward_kernel.astype(jnp.bfloat16), "fsdp", axis=1, tiled=True),
        lax.all_gather(output_kernel.astype(jnp.bfloat16), "fsdp", axis=2, tiled=True),
        lax.all_gather(embed_matrix.astype(jnp.bfloat16), "fsdp", axis=0, tiled=True),
    )
    target = residual_target[0]
    condition = conditioning[0]
    noise_cells = noise_sample[0]
    members_all = (
        lax.axis_size("fsdp")
        * target.shape[0]
        * target.shape[1]
        * lax.axis_size("rows")
        * target.shape[2]
    )
    sigma_level, skip_scale, out_scale, in_scale, weight = preconditions(noise_level[0])
    noisy = target + sigma_level * noise_cells
    stacked = jnp.concatenate([in_scale * noisy, condition], axis=0).astype(jnp.bfloat16)
    embedded = embedding(sigma_level, embed_taps.shape[0])
    level_shift = jnp.dot(embedded[None, :], embed_taps, preferred_element_type=jnp.float32)[0]
    act_a, pad_input = band_convolve(stacked, input_taps)
    hat_a, inv_a = norm_forward(act_a, GROUPS)
    raw_b, pad_first = band_convolve(activate(hat_a), first_taps)
    act_b = raw_b + level_shift[:, None, None]
    hat_b, inv_b = norm_forward(act_b, GROUPS)
    branch, pad_second = band_convolve(activate(hat_b), second_taps)
    fine_sum = act_a + branch
    pooled = pool_down(fine_sum).astype(jnp.bfloat16)
    act_c, pad_down = band_convolve(pooled, down_taps)
    hat_c, inv_c = norm_forward(act_c, GROUPS)
    coarse_branch, pad_coarse = band_convolve(activate(hat_c), coarse_taps)
    coarse = act_c + coarse_branch
    lifted = lift_up(coarse).astype(jnp.bfloat16)
    merged_raw, pad_upward = band_convolve(lifted, upward_taps)
    merged = merged_raw + fine_sum
    hat_d, inv_d = norm_forward(merged, GROUPS)
    fields, pad_output = band_convolve(activate(hat_d), output_taps)
    denoised = skip_scale * noisy + out_scale * fields
    mismatch = denoised - target
    loss_total = lax.psum(jnp.sum(weight * mismatch * mismatch), ("fsdp", "rows"))
    loss_value = loss_total / members_all
    grad_fields = (2.0 * weight * out_scale / members_all * mismatch).astype(jnp.bfloat16)
    output_grad = kernel_grad(pad_output, grad_fields)
    back_d, unused = band_convolve(grad_fields, transposed(output_taps))
    grad_merged = norm_backward(back_d, hat_d, inv_d, GROUPS)
    merged_low = grad_merged.astype(jnp.bfloat16)
    upward_grad = kernel_grad(pad_upward, merged_low)
    back_lift, unused = band_convolve(merged_low, transposed(upward_taps))
    grad_coarse = lift_back(back_lift)
    coarse_low = grad_coarse.astype(jnp.bfloat16)
    coarse_grad = kernel_grad(pad_coarse, coarse_low)
    back_c, unused = band_convolve(coarse_low, transposed(coarse_taps))
    grad_act_c = grad_coarse + norm_backward(back_c, hat_c, inv_c, GROUPS)
    act_c_low = grad_act_c.astype(jnp.bfloat16)
    down_grad = kernel_grad(pad_down, act_c_low)
    back_pool, unused = band_convolve(act_c_low, transposed(down_taps))
    grad_fine = grad_merged + 0.25 * lift_up(back_pool)
    fine_low = grad_fine.astype(jnp.bfloat16)
    second_grad = kernel_grad(pad_second, fine_low)
    back_b, unused = band_convolve(fine_low, transposed(second_taps))
    grad_act_b = norm_backward(back_b, hat_b, inv_b, GROUPS)
    act_b_low = grad_act_b.astype(jnp.bfloat16)
    first_grad = kernel_grad(pad_first, act_b_low)
    embed_grad = embedded.astype(jnp.float32)[:, None] * jnp.sum(grad_act_b, axis=(1, 2))[None, :]
    back_a, unused = band_convolve(act_b_low, transposed(first_taps))
    grad_act_a = grad_fine + norm_backward(back_a, hat_a, inv_a, GROUPS)
    input_grad = kernel_grad(pad_input, grad_act_a.astype(jnp.bfloat16))
    gradients = (
        input_grad,
        first_grad,
        second_grad,
        down_grad,
        coarse_grad,
        upward_grad,
        output_grad,
        embed_grad,
    )
    band_sums = (
        lax.psum(gradients[0].astype(jnp.bfloat16), "rows").astype(jnp.float32),
        lax.psum(gradients[1].astype(jnp.bfloat16), "rows").astype(jnp.float32),
        lax.psum(gradients[2].astype(jnp.bfloat16), "rows").astype(jnp.float32),
        lax.psum(gradients[3].astype(jnp.bfloat16), "rows").astype(jnp.float32),
        lax.psum(gradients[4].astype(jnp.bfloat16), "rows").astype(jnp.float32),
        lax.psum(gradients[5].astype(jnp.bfloat16), "rows").astype(jnp.float32),
        lax.psum(gradients[6].astype(jnp.bfloat16), "rows").astype(jnp.float32),
        lax.psum(gradients[7].astype(jnp.bfloat16), "rows").astype(jnp.float32),
    )
    shards = (
        lax.psum_scatter(
            band_sums[0].astype(jnp.bfloat16), "fsdp", scatter_dimension=1, tiled=True
        ).astype(jnp.float32),
        lax.psum_scatter(
            band_sums[1].astype(jnp.bfloat16), "fsdp", scatter_dimension=1, tiled=True
        ).astype(jnp.float32),
        lax.psum_scatter(
            band_sums[2].astype(jnp.bfloat16), "fsdp", scatter_dimension=1, tiled=True
        ).astype(jnp.float32),
        lax.psum_scatter(
            band_sums[3].astype(jnp.bfloat16), "fsdp", scatter_dimension=1, tiled=True
        ).astype(jnp.float32),
        lax.psum_scatter(
            band_sums[4].astype(jnp.bfloat16), "fsdp", scatter_dimension=1, tiled=True
        ).astype(jnp.float32),
        lax.psum_scatter(
            band_sums[5].astype(jnp.bfloat16), "fsdp", scatter_dimension=1, tiled=True
        ).astype(jnp.float32),
        lax.psum_scatter(
            band_sums[6].astype(jnp.bfloat16), "fsdp", scatter_dimension=2, tiled=True
        ).astype(jnp.float32),
        lax.psum_scatter(
            band_sums[7].astype(jnp.bfloat16), "fsdp", scatter_dimension=0, tiled=True
        ).astype(jnp.float32),
    )
    denoised_out = denoised[None]
    return (
        denoised_out,
        loss_value,
        shards[0],
        shards[1],
        shards[2],
        shards[3],
        shards[4],
        shards[5],
        shards[6],
        shards[7],
    )


def solution(mesh):
    in_specs = (
        P("fsdp", None, "rows", None),
        P("fsdp", None, "rows", None),
        P("fsdp", None, "rows", None),
        P("fsdp"),
        P(None, "fsdp", None),
        P(None, "fsdp", None),
        P(None, "fsdp", None),
        P(None, "fsdp", None),
        P(None, "fsdp", None),
        P(None, "fsdp", None),
        P(None, None, "fsdp"),
        P("fsdp", None),
    )
    out_specs = (
        P("fsdp", None, "rows", None),
        P(),
        P(None, "fsdp", None),
        P(None, "fsdp", None),
        P(None, "fsdp", None),
        P(None, "fsdp", None),
        P(None, "fsdp", None),
        P(None, "fsdp", None),
        P(None, None, "fsdp"),
        P("fsdp", None),
    )
    return jax.shard_map(
        per_device, mesh=mesh, in_specs=in_specs, out_specs=out_specs, check_vma=False
    )
```

profile of v0, /device:TPU:0, one launch (start us, length us, event | category | flops | bytes accessed | tf_op | source)
XLA Modules:
  0.0 813.7 jit_solution(9418838502122393676)
XLA Ops:
  16.1 5.3 all_gather.25
  21.4 5.1 all_gather.30
  26.6 6.9 all_gather.24
  35.2 6.1 all_gather.29
  42.8 4.4 all_gather.26
  51.7 31.2 %all-reduce.20 = (f32[32]{0:T(128)S(1)}, f32[32]{0:T(128)S(1)}) all-reduce(f32[32]{0:T(128)S(1)} %reduce_sum.230, f32[32]{0:T(128)S(1)} %reduce_sum.224), channel_id=1, replica_groups=mesh['fsdp'=2,'rows'=16] {'rows'}, use_global_device_ids=true, to_apply=%region_5.6 | all-reduce | flops 64 | bytes 512 | tf_op jit(solution)/shard_map/psum | solution.py:89
  87.7 9.7 %all_gather.28 = bf16[9,128,64]{2,0,1:T(8,128)(2,1)S(1)} all-gather(bf16[9,64,64]{2,0,1:T(8,128)(2,1)S(1)} %copy.299), channel_id=1, replica_groups=mesh['fsdp'=2,'rows'=16] {'fsdp'}, dimensions={1}, use_global_device_ids=true | all-gather | bytes 221184 | tf_op jit(solution)/shard_map/all_gather | solution.py:163
  98.3 5.1 all_gather.27
  108.2 29.5 %all-reduce.19 = (f32[32]{0:T(128)S(1)}, f32[32]{0:T(128)S(1)}) all-reduce(f32[32]{0:T(128)S(1)} %reduce_sum.239, f32[32]{0:T(128)S(1)} %reduce_sum.233), channel_id=1, replica_groups=mesh['fsdp'=2,'rows'=16] {'rows'}, use_global_device_ids=true, to_apply=%region_11.12 | all-reduce | flops 64 | bytes 512 | tf_op jit(solution)/shard_map/psum | solution.py:89
  148.8 3.4 reduce_sum.240
  152.4 4.4 collective-permute-start.6
  159.1 6.9 all_gather.31
  169.7 29.6 %all-reduce.18 = (f32[32]{0:T(128)S(1)}, f32[32]{0:T(128)S(1)}) all-reduce(f32[32]{0:T(128)S(1)} %reduce_sum.252, f32[32]{0:T(128)S(1)} %reduce_sum.246), channel_id=1, replica_groups=mesh['fsdp'=2,'rows'=16] {'rows'}, use_global_device_ids=true, to_apply=%region_18.19 | all-reduce | flops 64 | bytes 512 | tf_op jit(solution)/shard_map/psum | solution.py:89
  208.4 4.4 collective-permute-start.10
  222.8 32.5 %all-reduce.17 = (f32[32]{0:T(128)S(1)}, f32[32]{0:T(128)S(1)}) all-reduce(f32[32]{0:T(128)S(1)} %reduce_sum.261, f32[32]{0:T(128)S(1)} %reduce_sum.255), channel_id=1, replica_groups=mesh['fsdp'=2,'rows'=16] {'rows'}, use_global_device_ids=true, to_apply=%region_24.25 | all-reduce | flops 64 | bytes 512 | tf_op jit(solution)/shard_map/psum | solution.py:89
  279.9 31.3 %all-reduce.16 = (f32[32]{0:T(128)S(1)}, f32[32]{0:T(128)S(1)}) all-reduce(f32[32]{0:T(128)S(1)} %reduce_sum.323, f32[32]{0:T(128)S(1)} %reduce_sum.320), channel_id=1, replica_groups=mesh['fsdp'=2,'rows'=16] {'rows'}, use_global_device_ids=true, to_apply=%region_32.33 | all-reduce | flops 64 | bytes 512 | tf_op jit(solution)/shard_map/psum | solution.py:110
  311.6 2.9 fusion.607
  328.1 3.9 reduce_sum.324
  333.2 3.0 collective-permute-start.18
  343.3 32.0 %all-reduce.15 = (f32[32]{0:T(128)S(1)}, f32[32]{0:T(128)S(1)}) all-reduce(f32[32]{0:T(128)S(1)} %reduce_sum.330, f32[32]{0:T(128)S(1)} %reduce_sum.327), channel_id=1, replica_groups=mesh['fsdp'=2,'rows'=16] {'rows'}, use_global_device_ids=true, to_apply=%region_39.40 | all-reduce | flops 64 | bytes 512 | tf_op jit(solution)/shard_map/psum | solution.py:110
  391.3 3.2 copy.347
  394.4 2.9 fusion.606
  397.6 3.0 collective-permute-start.22
  415.9 32.4 %all-reduce.14 = (f32[32]{0:T(128)}, f32[32]{0:T(128)}) all-reduce(f32[32]{0:T(128)} %reduce_sum.336, f32[32]{0:T(128)} %reduce_sum.333), channel_id=1, replica_groups=mesh['fsdp'=2,'rows'=16] {'rows'}, use_global_device_ids=true, to_apply=%region_45.46 | all-reduce | flops 64 | bytes 512 | tf_op jit(solution)/shard_map/psum | solution.py:110
  473.9 30.8 %all-reduce.13 = (f32[32]{0:T(128)}, f32[32]{0:T(128)}) all-reduce(f32[32]{0:T(128)} %reduce_sum.342, f32[32]{0:T(128)} %reduce_sum.339), channel_id=1, replica_groups=mesh['fsdp'=2,'rows'=16] {'rows'}, use_global_device_ids=true, to_apply=%region_51.52 | all-reduce | flops 64 | bytes 512 | tf_op jit(solution)/shard_map/psum | solution.py:110
  556.4 13.2 %reduce-scatter.15.cloned.1.call-done = bf16[9,32,64]{2,1,0:T(8,128)(2,1)} async-done(((bf16[9,64,64]{2,1,0:T(8,128)(2,1)}), bf16[9,32,64]{2,1,0:T(8,128)(2,1)}) %reduce-scatter.15.cloned.1.call-update) | async-done | bytes 36880 | tf_op jit(solution)/shard_map/reduce_scatter | solution.py:255
  569.6 13.2 %reduce-scatter.27.cloned.1.call-done = bf16[64,576]{1,0:T(8,128)(2,1)} async-done(((bf16[128,576]{1,0:T(8,128)(2,1)}), bf16[64,576]{1,0:T(8,128)(2,1)}) %reduce-scatter.27.cloned.1.call-update) | async-done | bytes 73744
  584.8 10.8 %reduce-scatter.21.cloned.1.call-done = bf16[9,32,128]{2,1,0:T(8,128)(2,1)} async-done(((bf16[9,64,128]{2,1,0:T(8,128)(2,1)}), bf16[9,32,128]{2,1,0:T(8,128)(2,1)}) %reduce-scatter.21.cloned.1.call-update) | async-done | bytes 73744 | tf_op jit(solution)/shard_map/reduce_scatter | solution.py:267
  595.6 14.9 %reduce-scatter.19.cloned.1.call-done = bf16[9,64,128]{2,1,0:T(8,128)(2,1)} async-done(((bf16[9,128,128]{2,1,0:T(8,128)(2,1)}), bf16[9,64,128]{2,1,0:T(8,128)(2,1)}) %reduce-scatter.19.cloned.1.call-update) | async-done | bytes 147472 | tf_op jit(solution)/shard_map/reduce_scatter | solution.py:264
  610.5 39.7 %psum.183 = f32[]{:T(128)} all-reduce(f32[]{:T(128)} %get-tuple-element.111), channel_id=1, replica_groups=mesh['fsdp'=2,'rows'=16] {'fsdp','rows'}, use_global_device_ids=true, to_apply=%region_26.27 | all-reduce | flops 1 | bytes 8 | tf_op jit(solution)/shard_map/psum | solution.py:203
  651.6 53.7 %all-reduce.26.cloned.1.call-done = (bf16[9,32,24]{1,2,0:T(8,128)(2,1)}, bf16[9,32,64]{2,1,0:T(8,128)(2,1)}, bf16[9,32,64]{2,1,0:T(8,128)(2,1)}, bf16[9,12,32]{2,1,0:T(8,128)(2,1)}, bf16[64,64]{1,0:T(8,128)(2,1)}) async-done(((bf16[9,32,24]{1,2,0:T(8,128)(2,1)}, bf16[9,32,64]{2,1,0:T(8,128)(2,1)}, bf16[9,32,64]{2,1,0:T(8,128)(2,1)}, bf16[9,12,32]{2,1,0:T(8,128)(2,1)}, bf16[64,64]{1,0:T(8,128)(2,1)}), ...) | async-done | bytes 102672 | tf_op jit(solution)/shard_map/psum | solution.py:242
  712.6 87.7 %all-reduce.28.cloned.1.call-done = (bf16[9,64,64]{1,2,0:T(8,128)(2,1)}, bf16[9,64,128]{2,1,0:T(8,128)(2,1)}, bf16[9,32,128]{2,1,0:T(8,128)(2,1)}) async-done(((bf16[9,64,64]{1,2,0:T(8,128)(2,1)}, bf16[9,64,128]{2,1,0:T(8,128)(2,1)}, bf16[9,32,128]{2,1,0:T(8,128)(2,1)}), (bf16[9,64,64]{1,2,0:T(8,128)(2,1)}, bf16[9,64,128]{2,1,0:T(8,128)(2,1)}, bf16[9,32,128]{2,1,0:T(8,128)(2,1)})) %all-reduce.28.cloned.1.call-update) | async-done | bytes 294928 | tf_op jit(solution)/shard_map/psum | solution.py:245
  (618 shorter events, 230.6 us)
Async XLA Ops:
  7.2 543.4 %reduce-scatter.29.cloned.1.call-start = ((), (), s32[]{:S(2)}) async-start(), calls=%async_computation.15 | async-start | bytes 24576
  10.4 36.9 %collective-permute-start = (bf16[24,1,512]{2,0,1:T(8,128)(2,1)S(1)}, bf16[24,1,512]{2,0,1:T(8,128)(2,1)S(1)}, u32[]{:S(2)}, u32[]{:S(2)}) collective-permute-start(bf16[24,1,512]{2,0,1:T(8,128)(2,1)S(1)} %get-tuple-element.127), channel_id=1, source_target_pairs={{0,1},{1,2},{2,3},{3,4},{4,5},{5,6},{6,7},{7,8},{8,9},{9,10},{10,1... | collective-permute-start | bytes 73736 | tf_op jit(solution)/shard_map/ppermute | solution.py:22
  12.9 34.4 %collective-permute-start.1 = (bf16[24,1,512]{2,0,1:T(8,128)(2,1)S(1)}, bf16[24,1,512]{2,0,1:T(8,128)(2,1)S(1)}, u32[]{:S(2)}, u32[]{:S(2)}) collective-permute-start(bf16[24,1,512]{2,0,1:T(8,128)(2,1)S(1)} %get-tuple-element.128), channel_id=1, source_target_pairs={{1,0},{2,1},{3,2},{4,3},{5,4},{6,5},{7,6},{8,7},{9,8},{10,9},{11,1... | collective-permute-start | bytes 73736 | tf_op jit(solution)/shard_map/ppermute | solution.py:25
  83.7 19.8 %collective-permute-start.2 = (bf16[64,1,512]{2,0,1:T(8,128)(2,1)S(1)}, bf16[64,1,512]{2,0,1:T(8,128)(2,1)S(1)}, u32[]{:S(2)}, u32[]{:S(2)}) collective-permute-start(bf16[64,1,512]{2,0,1:T(8,128)(2,1)S(1)} %get-tuple-element.108), channel_id=1, source_target_pairs={{0,1},{1,2},{2,3},{3,4},{4,5},{5,6},{6,7},{7,8},{8,9},{9,10},{10,1... | collective-permute-start | bytes 196616 | tf_op jit(solution)/shard_map/ppermute | solution.py:22
  86.0 17.5 %collective-permute-start.3 = (bf16[64,1,512]{2,0,1:T(8,128)(2,1)S(1)}, bf16[64,1,512]{2,0,1:T(8,128)(2,1)S(1)}, u32[]{:S(2)}, u32[]{:S(2)}) collective-permute-start(bf16[64,1,512]{2,0,1:T(8,128)(2,1)S(1)} %get-tuple-element.109), channel_id=1, source_target_pairs={{1,0},{2,1},{3,2},{4,3},{5,4},{6,5},{7,6},{8,7},{9,8},{10,9},{11,1... | collective-permute-start | bytes 196616 | tf_op jit(solution)/shard_map/ppermute | solution.py:25
  138.5 4.9 collective-permute-start.4
  140.3 3.1 collective-permute-start.5
  152.4 13.8 %collective-permute-start.6 = (bf16[64,1,256]{2,0,1:T(8,128)(2,1)S(1)}, bf16[64,1,256]{2,0,1:T(8,128)(2,1)S(1)}, u32[]{:S(2)}, u32[]{:S(2)}) collective-permute-start(bf16[64,1,256]{2,0,1:T(8,128)(2,1)S(1)} %get-tuple-element.131), channel_id=1, source_target_pairs={{0,1},{1,2},{2,3},{3,4},{4,5},{5,6},{6,7},{7,8},{8,9},{9,10},{10,1... | collective-permute-start | bytes 98312 | tf_op jit(solution)/shard_map/ppermute | solution.py:22
  156.8 9.4 %collective-permute-start.7 = (bf16[64,1,256]{2,0,1:T(8,128)(2,1)S(1)}, bf16[64,1,256]{2,0,1:T(8,128)(2,1)S(1)}, u32[]{:S(2)}, u32[]{:S(2)}) collective-permute-start(bf16[64,1,256]{2,0,1:T(8,128)(2,1)S(1)} %get-tuple-element.132), channel_id=1, source_target_pairs={{1,0},{2,1},{3,2},{4,3},{5,4},{6,5},{7,6},{8,7},{9,8},{10,9},{11,1... | collective-permute-start | bytes 98312 | tf_op jit(solution)/shard_map/ppermute | solution.py:25
  201.5 3.1 collective-permute-start.9
  208.4 6.4 collective-permute-start.10
  212.8 3.2 collective-permute-start.11
  257.4 3.3 collective-permute-start.12
  266.6 6.9 collective-permute-start.14
  268.8 4.8 collective-permute-start.15
  273.5 278.7 %reduce-scatter.25.cloned.1.call-start = ((), (), s32[]{:S(2)}) async-start(), calls=%async_computation.13 | async-start | bytes 49152
  315.0 5.7 collective-permute-start.16
  316.3 5.1 collective-permute-start.17
  333.2 5.4 collective-permute-start.18
  378.4 5.2 collective-permute-start.20
  379.7 3.9 collective-permute-start.21
  397.6 6.3 collective-permute-start.22
  400.7 3.3 collective-permute-start.23
  457.4 3.9 collective-permute-start.24
  523.4 30.5 %reduce-scatter.23.cloned.1.call-start = ((), (), s32[]{:S(2)}) async-start(), calls=%async_computation.12 | async-start | bytes 49152 | tf_op jit(solution)/shard_map/reduce_scatter | solution.py:273
  524.9 31.6 %reduce-scatter.17.cloned.1.call-start = ((), (), s32[]{:S(2)}) async-start(), calls=%async_computation.9 | async-start | bytes 221184 | tf_op jit(solution)/shard_map/reduce_scatter | solution.py:258
  527.2 42.4 %reduce-scatter.15.cloned.1.call-start = ((), (), s32[]{:S(2)}) async-start(), calls=%async_computation.8 | async-start | bytes 221184 | tf_op jit(solution)/shard_map/reduce_scatter | solution.py:255
  539.1 43.7 %reduce-scatter.27.cloned.1.call-start = ((), (), s32[]{:S(2)}) async-start(), calls=%async_computation.14 | async-start | bytes 245760
  542.8 52.8 %reduce-scatter.21.cloned.1.call-start = ((), (), s32[]{:S(2)}) async-start(), calls=%async_computation.11 | async-start | bytes 221184 | tf_op jit(solution)/shard_map/reduce_scatter | solution.py:267
  546.2 64.3 %reduce-scatter.19.cloned.1.call-start = ((), (), s32[]{:S(2)}) async-start(), calls=%async_computation.10 | async-start | bytes 442368 | tf_op jit(solution)/shard_map/reduce_scatter | solution.py:264
  550.5 154.8 %all-reduce.26.cloned.1.call-start = ((), (), s32[]{:S(2)}) async-start(), calls=%async_computation.16 | async-start | bytes 512000 | tf_op jit(solution)/shard_map/psum | solution.py:242
  569.6 230.7 %all-reduce.28.cloned.1.call-start = ((), (), s32[]{:S(2)}) async-start(), calls=%async_computation.17 | async-start | bytes 737280 | tf_op jit(solution)/shard_map/psum | solution.py:245
  (99 other events, 1106.9 us)
Sparse Core Ops, SparseCore 0:
  273.6 9.7 reduce-scatter.28
  523.5 7.0 reduce-scatter.24
  533.4 9.8 reduce-scatter.22
  545.9 10.5 reduce-scatter.16
  559.1 10.4 reduce-scatter.14
  572.2 10.5 reduce-scatter.26
  585.1 10.4 reduce-scatter.20
  598.4 12.0 reduce-scatter.18
  615.6 89.6 all-reduce.25
  709.4 90.8 all-reduce.27
where the time goes:
time: 824 us; the launch traced here: 814 us
  blocking collectives  338 us (41%)
  waiting for transfers between devices  202 us (25%)
  matrix products  92.8 us (11%)
  local copies, waits for them, and re-layouts  57.7 us (7%)
  other arithmetic  54 us (7%)
  starting transfers between devices  48.7 us (6%)
  between operations  20.1 us (2%)
    psum x4, blocking collectives, norm_backward(): lax.psum((jnp.sum(grad_hat, axis=(1, 2, 3)), jnp.sum(grad_hat * hat_group...  126 us
    psum x4, blocking collectives, norm_forward(): lax.psum((jnp.sum(grouped, axis=(1, 2, 3)), jnp.sum(grouped * grouped, ax...  123 us
    psum x1, waiting for transfers between devices, per_device(): lax.psum(gradients[3].astype(jnp.bfloat16), 'rows').astype(jnp.float32)  87.7 us
    psum x1, waiting for transfers between devices, per_device(): lax.psum(gradients[0].astype(jnp.bfloat16), 'rows').astype(jnp.float32)  53.7 us
    dot_general x117, matrix products, tap_products(): jnp.einsum('oc,chw->ohw', kernels[position], window, preferred_element_ty...  51.4 us
    dot_general x63, matrix products, kernel_grad(): jnp.einsum('ohw,chw->oc', upstream, window, preferred_element_type=jnp.fl...  41.3 us
    psum x1, blocking collectives, per_device(): lax.psum(jnp.sum(weight * mismatch * mismatch), ('fsdp', 'rows'))  39.7 us
    ppermute x13, starting transfers between devices, padded_2(): lax.ppermute(lax.slice_in_dim(block, block.shape[dim] - width, None, axis...  30.5 us
  transfers between devices with their start and end apart: 36, of which 13 were waited for; matrix products, arithmetic and copies ran while one was open for 19% of the time, Pallas kernels for 0%

commit v1 on v0

v1 whole, which is shorter than its diff:
```python
import functools

import jax
import jax.numpy as jnp
from jax import lax
from jax.experimental import pallas as pl
from jax.experimental.pallas import tpu as pltpu
from jax.sharding import PartitionSpec as P

GROUPS = 32
STEPS = 64

sigma_low = 0.002
sigma_high = 80.0
sigma_data = 0.5
rho_power = 7.0
eps_norm = 1e-05

F32 = jnp.float32
BF16 = jnp.bfloat16

HALF = 256
ROWS = 8
CROWS = 4
FAR = 7


def preconditions(level_index):
    ramp_value = level_index.astype(jnp.float32) / (STEPS - 1)
    top_root = sigma_high ** (1.0 / rho_power)
    bottom = sigma_low ** (1.0 / rho_power)
    sigma_level = (top_root + ramp_value * (bottom - top_root)) ** rho_power
    sigma_total = sigma_level * sigma_level + sigma_data * sigma_data
    skip_scale = sigma_data * sigma_data / sigma_total
    out_scale = sigma_level * sigma_data * lax.rsqrt(sigma_total)
    in_scale = lax.rsqrt(sigma_total)
    weight = sigma_total / (sigma_level * sigma_data) ** 2
    return (sigma_level, skip_scale, out_scale, in_scale, weight)


def embedding(sigma_level, features):
    half_count = features // 2
    ramp_steps = jnp.arange(half_count, dtype=jnp.float32) / half_count
    frequency = 64.0 * 0.01**ramp_steps
    phase_angle = 0.25 * jnp.log(sigma_level) * frequency
    return jnp.concatenate([jnp.cos(phase_angle), jnp.sin(phase_angle)]).astype(jnp.bfloat16)


def row(ref, index):
    return ref[:, index * HALF : (index + 1) * HALF]


def put(ref, index, value):
    ref[:, index * HALF : (index + 1) * HALF] = value


def lane(shape):
    return lax.broadcasted_iota(jnp.int32, shape, 1)


def from_left(value):
    moved = pltpu.roll(value, 1, 1)
    return jnp.where(lane(value.shape) == 0, 0.0, moved)


def from_right(value):
    moved = pltpu.roll(value, value.shape[1] - 1, 1)
    return jnp.where(lane(value.shape) == value.shape[1] - 1, 0.0, moved)


def mm(left, right):
    return jnp.dot(left, right, preferred_element_type=F32)


def mm_nt(left, right):
    return lax.dot_general(left, right, (((1,), (1,)), ((), ())), preferred_element_type=F32)


def fine_taps(value):
    half = value.shape[0] // 2
    even, odd = value[:half], value[half:]
    return jnp.concatenate([from_left(odd), value, from_right(even)], axis=0).astype(BF16)


def coarse_taps(value):
    return jnp.concatenate([from_left(value), value, from_right(value)], axis=0).astype(BF16)


def fine_untap(taps):
    size = taps.shape[0] // 4
    even = taps[size : 2 * size] + from_left(taps[3 * size :])
    odd = taps[2 * size : 3 * size] + from_right(taps[:size])
    return jnp.concatenate([even, odd], axis=0)


def coarse_untap(taps):
    size = taps.shape[0] // 3
    return taps[size : 2 * size] + from_right(taps[:size]) + from_left(taps[2 * size :])


def spread(parts, first, last):
    out = {}
    for i in range(first, last + 1):
        size = parts[i - 1].shape[0] // 3
        out[i] = parts[i - 1][:size] + parts[i][size : 2 * size] + parts[i + 1][2 * size :]
    return out


def stack_rows(g, r):
    return jnp.concatenate([g[r + 1], g[r], g[r - 1]], axis=0)


def same_group(size, fine):
    left = lax.broadcasted_iota(jnp.int32, (size, size), 0)
    right = lax.broadcasted_iota(jnp.int32, (size, size), 1)
    if fine:
        half = size // 2
        left, right = left % half, right % half
        per = half // GROUPS
    else:
        per = size // GROUPS
    return left // per == right // per


def group_sums(stats_ref, fine):
    total = stats_ref[0]
    for index in range(1, stats_ref.shape[0]):
        total = total + stats_ref[index]
    member = same_group(128, fine)
    first = jnp.sum(jnp.where(member, total[0:1, :], 0.0), axis=1, keepdims=True)
    second = jnp.sum(jnp.where(member, total[1:2, :], 0.0), axis=1, keepdims=True)
    return first, second


def norm_columns(stats_ref, fine, members):
    first, second = group_sums(stats_ref, fine)
    mean = first / members
    inverse = lax.rsqrt(second / members - mean * mean + eps_norm)
    return mean, inverse


def back_columns(stats_ref, fine, members):
    first, second = group_sums(stats_ref, fine)
    return first / members, second / members


def to_row(column):
    size = column.shape[0]
    diagonal = lax.broadcasted_iota(jnp.int32, (size, size), 0) == lax.broadcasted_iota(
        jnp.int32, (size, size), 1
    )
    return jnp.sum(jnp.where(diagonal, column, 0.0), axis=0, keepdims=True)


def put_stats(ref, first, second):
    first = to_row(jnp.sum(first, axis=1, keepdims=True))
    second = to_row(jnp.sum(second, axis=1, keepdims=True))
    ref[...] = jnp.concatenate([first, second, jnp.zeros((6, 128), F32)], axis=0)


def silu(h):
    return h * (1.0 / (1.0 + jnp.exp(-h)))


def silu_slope(h):
    s = 1.0 / (1.0 + jnp.exp(-h))
    return s * (1.0 + h * (1.0 - s))


def masked(value, index, rows, scal):
    if index < 0:
        return value * scal[6]
    if index >= rows:
        return value * scal[7]
    return value


def pick(scal, when_odd, when_even):
    return jnp.where(scal[8] > 0.5, when_odd, when_even)


def spill(ref, value):
    for t in range(4):
        ref[t, : value.shape[0], :] = value[:, 128 * t : 128 * (t + 1)]


def strided(ref, index, size):
    return jnp.concatenate(
        [ref[t, pl.ds(index, size, stride=ROWS), :] for t in range(4)], axis=1
    )


def interleave(transposed):
    left = lax.broadcasted_iota(jnp.int32, (512, 512), 0)
    right = lax.broadcasted_iota(jnp.int32, (512, 512), 1)
    if transposed:
        left, right = right, left
    place = (left & 1) * HALF + (left >> 1)
    return jnp.where(place == right, 1.0, 0.0).astype(BF16)


def fine_grad(blocks, outs, ins):
    parts = []
    for a in range(3):
        even = blocks[(2 * a) * outs : (2 * a + 1) * outs]
        odd = blocks[(2 * a + 1) * outs : (2 * a + 2) * outs]
        parts.append(even[:, : 3 * ins] + odd[:, ins : 4 * ins])
    return jnp.concatenate(parts, axis=0).astype(BF16)


def place(width, target, offset):
    left = lax.broadcasted_iota(jnp.int32, (width, target), 0)
    right = lax.broadcasted_iota(jnp.int32, (width, target), 1)
    return jnp.where(left + offset == right, 1.0, 0.0).astype(BF16)


def flipped(value):
    size = value.shape[1]
    return mm_nt(place(size, size, 0), value).astype(BF16)


def fine_matrix(ref, outs, ins, slot):
    rows = []
    for a in range(3):
        total = None
        for b in range(3):
            tap = ref[(3 * a + b) * outs : (3 * a + b + 1) * outs, :ins]
            spot = jnp.concatenate(
                [place(ins, 4 * slot, b * slot), place(ins, 4 * slot, (b + 1) * slot)], axis=1
            )
            term = mm(tap, spot)
            total = term if total is None else total + term
        rows += [total[:, : 4 * slot], total[:, 4 * slot :]]
    return jnp.concatenate(rows, axis=0).astype(BF16)


def prepare_first(in_ref, first_ref, emb_ref, vec_ref, win, wfirst, wfirst_t, shift):
    win[...] = fine_matrix(in_ref, 64, 24, 32)
    first = fine_matrix(first_ref, 64, 64, 64)
    wfirst[...] = first
    wfirst_t[...] = flipped(first)
    line = mm(vec_ref[...], emb_ref[...])[0:1, :]
    both = jnp.concatenate([line, line], axis=1)
    diagonal = place(128, 128, 0).astype(F32)
    shift[...] = jnp.broadcast_to(
        jnp.sum(diagonal * both, axis=1, keepdims=True), (128, 128)
    )


def prepare_rest(
    second_ref, down_ref, coarse_ref, up_ref, out_ref,
    wsecond, wsecond_t, wdown, wdown_t, wcoarse, wcoarse_t, wup, wup_t, wout, wout_t,
):
    second = fine_matrix(second_ref, 64, 64, 64)
    wsecond[...] = second
    wsecond_t[...] = flipped(second)
    rows = []
    for a in range(3):
        total = None
        for b in range(3):
            tap = down_ref[(3 * a + b) * 128 : (3 * a + b + 1) * 128, :]
            term = mm(tap, place(64, 256, 64 * b))
            total = term if total is None else total + term
        rows.append(total)
    down = jnp.concatenate(rows, axis=0)[:, :192].astype(BF16)
    wdown[...] = down
    wdown_t[...] = flipped(down)
    rows = []
    for a in range(3):
        rows.append(
            jnp.concatenate(
                [coarse_ref[(3 * a + b) * 128 : (3 * a + b + 1) * 128, :] for b in range(3)], axis=1
            )
        )
    coarse = jnp.concatenate(rows, axis=0)
    wcoarse[...] = coarse
    wcoarse_t[...] = flipped(coarse)
    rows = []
    blank = jnp.zeros((64, 128), BF16)
    for a in range(3):
        taps = [up_ref[(3 * a + b) * 64 : (3 * a + b + 1) * 64, :] for b in range(3)]
        rows.append(jnp.concatenate(taps + [blank], axis=1))
        rows.append(jnp.concatenate([blank] + taps, axis=1))
    up = jnp.concatenate(rows, axis=0)
    wup[...] = up
    wup_t[...] = flipped(up)
    out = fine_matrix(out_ref, 16, 64, 64)
    wout[...] = out
    wout_t[...] = flipped(out)


def enter(scal, target, condition, noise, own, edge_a, edge_b, line_a, line_b, scratch):
    sigma, skip, in_scale = scal[0], scal[1], scal[3]
    noisy = target[...] + sigma * noise[...]
    q = skip * noisy - target[...]
    natural = jnp.concatenate([in_scale * noisy, condition[...]], axis=0).astype(BF16)
    spill(scratch, mm(natural, interleave(False)))
    blank = jnp.zeros((8, 512), F32)
    for i in range(ROWS):
        value = strided(scratch, i, 24)
        own[:, i * 512 : (i + 1) * 512] = jnp.concatenate([value, blank], axis=0).astype(BF16)
    top, low = own[:, : FAR * 512], own[:, (ROWS - FAR) * 512 :]
    edge_a[...] = pick(scal, top, low)
    edge_b[...] = pick(scal, low, top)
    spill(scratch, q)
    blank = jnp.zeros((4, 512), F32)
    top = jnp.concatenate([strided(scratch, 0, 12), blank], axis=0)
    low = jnp.concatenate([strided(scratch, ROWS - 1, 12), blank], axis=0)
    line_a[...] = pick(scal, top, low)
    line_b[...] = pick(scal, low, top)


def stage_a(scal, own, got_a, got_b, win, act, stats, kept, above, below):
    above[...] = pick(scal, got_a[...], got_b[...])
    below[...] = pick(scal, got_b[...], got_a[...])
    parts = {}
    total = jnp.zeros((128, HALF), F32)
    square = jnp.zeros((128, HALF), F32)
    for r in range(-FAR, ROWS + FAR):
        if r < 0:
            value = above[:, (r + FAR) * 512 : (r + FAR + 1) * 512]
        elif r < ROWS:
            value = own[:, r * 512 : (r + 1) * 512]
        else:
            value = below[:, (r - ROWS) * 512 : (r - ROWS + 1) * 512]
        value = value.astype(F32)
        z = fine_taps(jnp.concatenate([value[:, :HALF], value[:, HALF:]], axis=0))
        if -1 <= r <= ROWS:
            put(kept, r + 1, z)
        parts[r] = mm(win[...], z)
        i = r - 1
        if i > -FAR:
            value = spread(parts, i, i)[i]
            put(act, i + FAR - 1, value)
            del parts[i - 1]
            if 0 <= i < ROWS:
                total = total + value
                square = square + value * value
    put_stats(stats, total, square)


def stage_b(members, scal, act_a, stats_a, wfirst, shift, act_b, stats, kept):
    mean, inverse = norm_columns(stats_a, True, members)
    lift = shift[:, 0:1]
    parts = {}
    total = jnp.zeros((128, HALF), F32)
    square = jnp.zeros((128, HALF), F32)
    for r in range(-6, ROWS + 6):
        value = silu((row(act_a, r + 6) - mean) * inverse)
        z = fine_taps(masked(value, r, ROWS, scal))
        if 0 <= r < ROWS:
            put(kept, r, z)
        parts[r] = mm(wfirst[...], z)
        i = r - 1
        if i > -6:
            value = spread(parts, i, i)[i] + lift
            put(act_b, i + 5, value)
            del parts[i - 1]
            if 0 <= i < ROWS:
                total = total + value
                square = square + value * value
    put_stats(stats, total, square)


def stage_c(
    members, scal, act_a, act_b, stats_b, wsecond, wdown,
    fine, act_c, edge, stats, kept, kept_pool,
):
    mean, inverse = norm_columns(stats_b, True, members)
    parts = {}
    pooled = {}
    half = {}
    for r in range(-5, ROWS + 5):
        value = silu((row(act_b, r + 5) - mean) * inverse)
        z = fine_taps(masked(value, r, ROWS, scal))
        if 0 <= r < ROWS:
            put(kept, r, z)
        parts[r] = mm(wsecond[...], z)
        i = r - 1
        if i > -5:
            value = spread(parts, i, i)[i] + row(act_a, i + 6)
            put(fine, i + 4, value)
            del parts[i - 1]
            half[i] = value[:64] + value[64:]
            if i % 2:
                value = 0.25 * (half.pop(i - 1) + half.pop(i))
                value = masked(value, i // 2, CROWS, scal)
                pooled[i // 2] = value.astype(BF16).astype(F32)
    parts = {}
    total = jnp.zeros((128, HALF), F32)
    square = jnp.zeros((128, HALF), F32)
    for r in range(-2, CROWS + 2):
        z = coarse_taps(pooled[r])
        if 0 <= r < CROWS:
            put(kept_pool, r, z)
        parts[r] = mm(wdown[...], z)
        i = r - 1
        if i > -2:
            value = spread(parts, i, i)[i]
            put(act_c, i + 1, value)
            del parts[i - 1]
            if 0 <= i < CROWS:
                total = total + value
                square = square + value * value
            if i in (1, 2):
                put(edge, i - 1, value)
    put_stats(stats, total, square)


def stage_d(
    members, scal, act_c, got_a, got_b, stats_c, wcoarse, wup, fine,
    merged, wide_c, stats, kept_c, kept_up, ring,
):
    mean, inverse = norm_columns(stats_c, False, members)
    for j in range(2):
        put(ring, j, pick(scal, row(got_a, j), row(got_b, j)))
        put(ring, CROWS + 4 + j, pick(scal, row(got_b, j), row(got_a, j)))
    for j in range(CROWS + 2):
        put(ring, j + 2, row(act_c, j))
    parts = {}
    lifted = {}
    for r in range(-3, CROWS + 3):
        value = silu((row(ring, r + 3) - mean) * inverse)
        z = coarse_taps(masked(value, r, CROWS, scal))
        if 0 <= r < CROWS:
            put(kept_c, r, z)
        parts[r] = mm(wcoarse[...], z)
        i = r - 1
        if i > -3:
            value = spread(parts, i, i)[i] + row(ring, i + 3)
            put(wide_c, i + 2, row(ring, i + 3))
            del parts[i - 1]
            lifted[i] = masked(value, i, CROWS, scal).astype(BF16).astype(F32)
    parts = {}
    total = jnp.zeros((128, HALF), F32)
    square = jnp.zeros((128, HALF), F32)
    for r in range(-2, CROWS + 2):
        z = coarse_taps(lifted[r])
        if 0 <= r < CROWS:
            put(kept_up, r, z)
        four = jnp.concatenate([z[:128], z[128:256], z[128:256], z[256:]], axis=0)
        parts[2 * r] = parts[2 * r + 1] = mm(wup[...], four)
        for i in (2 * r - 1, 2 * r):
            if i >= -3:
                value = spread(parts, i, i)[i] + row(fine, i + 4)
                put(merged, i + 3, value)
                parts.pop(i - 1)
                if 0 <= i < ROWS:
                    total = total + value
                    square = square + value * value
    put_stats(stats, total, square)


def stage_out(
    members, scal, merged, stats_d, wout, wout_t, target, noise, line_a, line_b,
    denoised, loss, back, edge_a, edge_b, stats, grad, pairs, cells, gs, zs,
    goals, noisies, found,
):
    sigma, skip, out_scale, weight, coef = scal[0], scal[1], scal[2], scal[4], scal[5]
    mean, inverse = norm_columns(stats_d, True, members)
    parts = {}
    for r in range(-2, ROWS + 2):
        value = silu((row(merged, r + 3) - mean) * inverse)
        z = fine_taps(masked(value, r, ROWS, scal))
        if 0 <= r < ROWS:
            put(zs, r, z)
        parts[r] = mm(wout[...], z)
        i = r - 1
        if i > -2:
            value = spread(parts, i, i)[i]
            del parts[i - 1]
            pairs[16 * (i + 1) : 16 * (i + 2), :] = jnp.concatenate(
                [value[:16], value[16:]], axis=1
            )
    value = pairs[...]
    high = value.astype(BF16)
    low = (value - high.astype(F32)).astype(BF16)
    back_order = interleave(True)
    pairs[...] = mm(high, back_order) + mm(low, back_order)
    blank = jnp.zeros((4, 512), F32)
    loss_sum = jnp.zeros((12, 512), F32)
    top = pick(scal, line_a[...], line_b[...]) + out_scale * pairs[0:16, :]
    cells[0:16, :] = coef * scal[6] * top
    low = pick(scal, line_b[...], line_a[...]) + out_scale * pairs[16 * (ROWS + 1) :, :]
    cells[16 * (ROWS + 1) :, :] = coef * scal[7] * low
    spill(goals, target[...])
    spill(noisies, target[...] + sigma * noise[...])
    for i in range(ROWS):
        goal = strided(goals, i, 12)
        noisy = strided(noisies, i, 12)
        estimate = skip * noisy + out_scale * pairs[16 * (i + 1) : 16 * (i + 1) + 12, :]
        for t in range(4):
            found[t, pl.ds(i, 12, stride=ROWS), :] = estimate[:, 128 * t : 128 * (t + 1)]
        mismatch = estimate - goal
        loss_sum = loss_sum + weight * mismatch * mismatch
        cells[16 * (i + 1) : 16 * (i + 2), :] = jnp.concatenate([coef * mismatch, blank], axis=0)
    denoised[...] = jnp.concatenate([found[t] for t in range(4)], axis=1)
    loss[...] = jnp.broadcast_to(
        jnp.sum(jnp.sum(loss_sum, axis=1, keepdims=True), axis=0, keepdims=True), (8, 128)
    )
    pairs[...] = mm(cells[...].astype(BF16), interleave(False))
    g = {}
    for i in range(-1, ROWS + 1):
        value = pairs[16 * (i + 1) : 16 * (i + 2), :]
        g[i] = jnp.concatenate([value[:, :HALF], value[:, HALF:]], axis=0).astype(BF16)
    total = jnp.zeros((128, HALF), F32)
    cross = jnp.zeros((128, HALF), F32)
    for r in range(ROWS):
        rows = stack_rows(g, r)
        put(gs, r, rows)
        value = fine_untap(mm(wout_t[...], rows))
        put(back, r, value)
        hat = (row(merged, r + 3) - mean) * inverse
        e = value * silu_slope(hat)
        total = total + e
        cross = cross + e * hat
    put_stats(stats, total, cross)
    top, low = back[:, : 3 * HALF].astype(BF16), back[:, (ROWS - 3) * HALF :].astype(BF16)
    edge_a[...] = pick(scal, top, low)
    edge_b[...] = pick(scal, low, top)
    grad[...] = fine_grad(mm_nt(gs[...], zs[...]), 16, 64)


def stage_up(
    members, members_c, scal, merged, stats_d, stats_ed, back, got_a, got_b, kept_up, wup_t,
    act_c, stats_c, kept_c, wcoarse_t,
    grad_merged, back_c, grad_coarse, edge_a, edge_b, stats, grad_up, grad_c, gs, zs, gc,
):
    mean, inverse = norm_columns(stats_d, True, members)
    shift, slope = back_columns(stats_ed, True, members)
    g = {}
    for r in range(-3, ROWS + 3):
        hat = (row(merged, r + 3) - mean) * inverse
        if r < 0:
            u = pick(scal, row(got_a, r + 3), row(got_b, r + 3)).astype(F32)
        elif r < ROWS:
            u = row(back, r)
        else:
            u = pick(scal, row(got_b, r - ROWS), row(got_a, r - ROWS)).astype(F32)
        value = inverse * (u * silu_slope(hat) - shift - hat * slope)
        value = masked(value, r, ROWS, scal)
        if -2 <= r < ROWS + 2:
            put(grad_merged, r + 2, value)
        g[r] = value.astype(BF16)
    gk = {}
    half = {}
    for r in range(-2, ROWS + 2):
        rows = stack_rows(g, r)
        if 0 <= r < ROWS:
            put(gs, r, rows)
            put(zs, r, row(kept_up, r // 2))
        taps = mm(wup_t[...], rows)
        half[r] = taps[128:256] + taps[256:384] + from_right(taps[:128]) + from_left(taps[384:])
        if r % 2:
            value = masked(half.pop(r - 1) + half.pop(r), r // 2, CROWS, scal)
            put(grad_coarse, r // 2 + 1, value)
            gk[r // 2] = value.astype(BF16)
    blocks = mm_nt(gs[...], zs[...])
    parts = []
    for a in range(3):
        even = blocks[128 * a : 128 * a + 64]
        odd = blocks[128 * a + 64 : 128 * a + 128]
        parts.append(
            jnp.concatenate(
                [
                    even[:, :128] + odd[:, 128:256],
                    even[:, 128:256] + odd[:, 128:256],
                    even[:, 128:256] + odd[:, 256:],
                ],
                axis=1,
            )
        )
    grad_up[...] = jnp.concatenate(parts, axis=0).astype(BF16)
    mean, inverse = norm_columns(stats_c, False, members_c)
    total = jnp.zeros((128, HALF), F32)
    cross = jnp.zeros((128, HALF), F32)
    for r in range(CROWS):
        rows = stack_rows(gk, r)
        put(gc, r, rows)
        value = coarse_untap(mm(wcoarse_t[...], rows))
        put(back_c, r, value)
        hat = (row(act_c, r + 2) - mean) * inverse
        e = value * silu_slope(hat)
        total = total + e
        cross = cross + e * hat
    put_stats(stats, total, cross)
    grad_c[...] = mm_nt(gc[...], kept_c[...]).astype(BF16)
    top = [row(back_c, 0).astype(BF16), row(back_c, 1).astype(BF16), gk[1]]
    low = [row(back_c, 2).astype(BF16), row(back_c, 3).astype(BF16), gk[2]]
    for j in range(3):
        put(edge_a, j, pick(scal, top[j], low[j]))
        put(edge_b, j, pick(scal, low[j], top[j]))


def stage_down(
    members, members_c, scal, stats_c, stats_ec, act_c, back_c, grad_coarse, got_a, got_b,
    wdown_t, kept_pool, grad_merged, act_b, stats_b, kept_b, wsecond_t,
    grad_fine, back_b, stats, grad_down, grad_second, gs, gc,
):
    mean, inverse = norm_columns(stats_c, False, members_c)
    shift, slope = back_columns(stats_ec, False, members_c)
    g = {}
    for r in range(-2, CROWS + 2):
        hat = (row(act_c, r + 2) - mean) * inverse
        if r < 0:
            u = pick(scal, row(got_a, r + 2), row(got_b, r + 2)).astype(F32)
        elif r < CROWS:
            u = row(back_c, r)
        else:
            u = pick(scal, row(got_b, r - CROWS), row(got_a, r - CROWS)).astype(F32)
        if r == -2:
            through = pick(scal, row(got_a, 2), row(got_b, 2)).astype(F32)
        elif r == CROWS + 1:
            through = pick(scal, row(got_b, 2), row(got_a, 2)).astype(F32)
        else:
            through = row(grad_coarse, r + 1)
        value = through + inverse * (u * silu_slope(hat) - shift - hat * slope)
        g[r] = masked(value, r, CROWS, scal).astype(BF16)
    fine = {}
    for r in range(-1, CROWS + 1):
        rows = stack_rows(g, r)
        if 0 <= r < CROWS:
            put(gc, r, rows)
        value = 0.25 * coarse_untap(mm(wdown_t[...], rows))
        both = jnp.concatenate([value, value], axis=0)
        for i in (2 * r, 2 * r + 1):
            value = masked(row(grad_merged, i + 2) + both, i, ROWS, scal)
            if 0 <= i < ROWS:
                put(grad_fine, i, value)
            fine[i] = value.astype(BF16)
    grad_down[...] = mm_nt(gc[...], kept_pool[...]).astype(BF16)
    mean, inverse = norm_columns(stats_b, True, members)
    total = jnp.zeros((128, HALF), F32)
    cross = jnp.zeros((128, HALF), F32)
    for r in range(-1, ROWS + 1):
        rows = stack_rows(fine, r)
        value = fine_untap(mm(wsecond_t[...], rows))
        put(back_b, r + 1, value)
        if 0 <= r < ROWS:
            put(gs, r, rows)
            hat = (row(act_b, r + 5) - mean) * inverse
            e = value * silu_slope(hat)
            total = total + e
            cross = cross + e * hat
    put_stats(stats, total, cross)
    grad_second[...] = fine_grad(mm_nt(gs[...], kept_b[...]), 64, 64)


def stage_first(
    members, scal, stats_b, stats_eb, act_b, back_b, wfirst_t, act_a, stats_a, kept_a,
    back_a, stats, grad_first, cell_sums, gs,
):
    mean, inverse = norm_columns(stats_b, True, members)
    shift, slope = back_columns(stats_eb, True, members)
    g = {}
    sums = jnp.zeros((128, HALF), F32)
    for r in range(-1, ROWS + 1):
        hat = (row(act_b, r + 5) - mean) * inverse
        value = inverse * (row(back_b, r + 1) * silu_slope(hat) - shift - hat * slope)
        if 0 <= r < ROWS:
            sums = sums + value
        g[r] = masked(value, r, ROWS, scal).astype(BF16)
    line = to_row(jnp.sum(sums, axis=1, keepdims=True))
    cell_sums[...] = jnp.broadcast_to(line, (8, 128))
    mean, inverse = norm_columns(stats_a, True, members)
    total = jnp.zeros((128, HALF), F32)
    cross = jnp.zeros((128, HALF), F32)
    for r in range(ROWS):
        rows = stack_rows(g, r)
        put(gs, r, rows)
        value = fine_untap(mm(wfirst_t[...], rows))
        put(back_a, r, value)
        hat = (row(act_a, r + 6) - mean) * inverse
        e = value * silu_slope(hat)
        total = total + e
        cross = cross + e * hat
    put_stats(stats, total, cross)
    grad_first[...] = fine_grad(mm_nt(gs[...], kept_a[...]), 64, 64)


def stage_last(members, stats_a, stats_ea, act_a, back_a, grad_fine, kept_in, grad_in, gs):
    mean, inverse = norm_columns(stats_a, True, members)
    shift, slope = back_columns(stats_ea, True, members)
    for r in range(ROWS):
        hat = (row(act_a, r + 6) - mean) * inverse
        value = row(grad_fine, r) + inverse * (
            row(back_a, r) * silu_slope(hat) - shift - hat * slope
        )
        put(gs, r, value.astype(BF16))
    parts = []
    for a in range(3):
        blocks = mm_nt(gs[...], kept_in[:, a * HALF : (a + ROWS) * HALF])
        parts.append(blocks[:64, :96] + blocks[64:, 32:128])
    grad_in[...] = jnp.concatenate(parts, axis=0).astype(BF16)


def shape(rows, lanes, dtype=F32):
    return jax.ShapeDtypeStruct((rows, lanes), dtype)


def run(name, kernel, outs, scal, *operands, scratch=()):
    vmem = pl.BlockSpec(memory_space=pltpu.VMEM)
    specs = [vmem] * len(operands)
    if scal is not None:
        operands = (scal,) + operands
        specs = [pl.BlockSpec(memory_space=pltpu.SMEM)] + specs
    return pl.pallas_call(
        kernel,
        out_shape=tuple(outs),
        in_specs=specs,
        out_specs=tuple([vmem] * len(outs)),
        scratch_shapes=[pltpu.VMEM(dims, dtype) for dims, dtype in scratch],
        compiler_params=pltpu.CompilerParams(vmem_limit_bytes=56 * 1024 * 1024),
        name=name,
    )(*operands)


def sum_parts(stats):
    count = lax.axis_size("rows")
    return lax.all_to_all(jnp.broadcast_to(stats[None], (count,) + stats.shape), "rows", 0, 0)


def swap(value_a, value_b):
    count = lax.axis_size("rows")
    pairs = [(i, i ^ 1) for i in range(count)]
    across = []
    for i in range(1, count - 1, 2):
        across += [(i, i + 1), (i + 1, i)]
    return lax.ppermute(value_a, "rows", pairs), lax.ppermute(value_b, "rows", across)


def gather_kernels(shards, dims):
    count = lax.axis_size("fsdp")
    flat = jnp.concatenate([item.astype(BF16).reshape(-1) for item in shards])
    if count == 2:
        other = lax.ppermute(flat, "fsdp", [(0, 1), (1, 0)])
        low = lax.axis_index("fsdp") == 0
        pieces = [jnp.where(low, flat, other), jnp.where(low, other, flat)]
    else:
        whole = lax.all_gather(flat, "fsdp")
        pieces = [whole[i] for i in range(count)]
    outs = []
    start = 0
    for item, dim in zip(shards, dims):
        parts = [piece[start : start + item.size].reshape(item.shape) for piece in pieces]
        outs.append(jnp.concatenate(parts, axis=dim))
        start += item.size
    return outs


def reduce_gradients(grads):
    count, bands = lax.axis_size("fsdp"), lax.axis_size("rows")
    sizes = [item.shape[1] for item in grads]
    flat = jnp.concatenate(grads, axis=1)
    total = flat.shape[1]
    chunk = -(-total // (bands * 1024)) * 1024
    flat = jnp.pad(flat, ((0, 0), (0, chunk * bands - total)))
    flat = flat.reshape(count * bands, chunk // 128, 128)
    got = lax.all_to_all(flat, ("fsdp", "rows"), 0, 0)
    mine = jnp.sum(got.astype(F32), axis=0).astype(BF16)
    whole = lax.all_to_all(jnp.broadcast_to(mine[None], (bands,) + mine.shape), "rows", 0, 0)
    whole = whole.reshape(-1)
    outs = []
    start = 0
    for size in sizes:
        outs.append(whole[start : start + size])
        start += size
    return outs


def per_device(
    residual_target,
    conditioning,
    noise_sample,
    noise_level,
    input_kernel,
    first_kernel,
    second_kernel,
    down_kernel,
    coarse_kernel,
    upward_kernel,
    output_kernel,
    embed_matrix,
):
    bands, count = lax.axis_size("rows"), lax.axis_size("fsdp")
    members = 2 * ROWS * 2 * HALF * bands
    members_c = 4 * CROWS * HALF * bands
    members_all = count * residual_target.size * bands
    me = lax.axis_index("rows")
    sigma_level, skip_scale, out_scale, in_scale, weight = preconditions(noise_level[0])
    coef = 2.0 * weight * out_scale / members_all
    scal = jnp.stack(
        [
            sigma_level,
            skip_scale,
            out_scale,
            in_scale,
            weight,
            coef,
            (me > 0).astype(F32),
            (me < bands - 1).astype(F32),
            (me % 2).astype(F32),
        ]
    )
    embedded = embedding(sigma_level, embed_matrix.shape[0] * count)
    target = residual_target.reshape(12 * ROWS, 512)
    condition = conditioning.reshape(12 * ROWS, 512)
    noise = noise_sample.reshape(12 * ROWS, 512)

    far = shape(32, FAR * 512, BF16)
    own, edge_a, edge_b, line_a, line_b = run(
        "enter",
        enter,
        [shape(32, ROWS * 512, BF16), far, far, shape(16, 512), shape(16, 512)],
        scal,
        target,
        condition,
        noise,
        scratch=[((4, 192, 128), F32)],
    )
    got_a, got_b = swap(edge_a, edge_b)
    line_a, line_b = swap(line_a, line_b)

    win_k, first_k, emb_k = gather_kernels([input_kernel, first_kernel, embed_matrix], (1, 1, 0))
    second_k, down_k, coarse_k, up_k, out_k = gather_kernels(
        [second_kernel, down_kernel, coarse_kernel, upward_kernel, output_kernel], (1, 1, 1, 1, 2)
    )
    out_k = jnp.pad(out_k, ((0, 0), (0, 4), (0, 0)))

    def flat(item):
        return item.reshape(-1, item.shape[-1])

    vector = jnp.broadcast_to(embedded[None, :], (16, embedded.shape[0]))
    win, wfirst, wfirst_t, shift = run(
        "prepare_first",
        prepare_first,
        [shape(384, 128, BF16), shape(384, 256, BF16), shape(256, 384, BF16), shape(128, 128)],
        None,
        flat(win_k),
        flat(first_k),
        emb_k,
        vector,
    )
    (
        wsecond, wsecond_t, wdown, wdown_t, wcoarse, wcoarse_t, wup, wup_t, wout, wout_t
    ) = run(
        "prepare_rest",
        prepare_rest,
        [
            shape(384, 256, BF16), shape(256, 384, BF16),
            shape(384, 192, BF16), shape(192, 384, BF16),
            shape(384, 384, BF16), shape(384, 384, BF16),
            shape(384, 512, BF16), shape(512, 384, BF16),
            shape(96, 256, BF16), shape(256, 96, BF16),
        ],
        None,
        flat(second_k), flat(down_k), flat(coarse_k), flat(up_k), flat(out_k),
    )

    stat = shape(8, 128)
    act_a, stats_a, kept_in = run(
        "stage_a",
        stage_a,
        [shape(128, 20 * HALF), stat, shape(128, 10 * HALF, BF16)],
        scal,
        own, got_a, got_b, win,
        scratch=[((32, FAR * 512), BF16), ((32, FAR * 512), BF16)],
    )
    stats_a = sum_parts(stats_a)
    act_b, stats_b, kept_a = run(
        "stage_b",
        functools.partial(stage_b, members),
        [shape(128, 18 * HALF), stat, shape(256, 8 * HALF, BF16)],
        scal,
        act_a, stats_a, wfirst, shift,
    )
    stats_b = sum_parts(stats_b)
    fine, act_c, edge, stats_c, kept_b, kept_pool = run(
        "stage_c",
        functools.partial(stage_c, members),
        [
            shape(128, 16 * HALF), shape(128, 6 * HALF), shape(128, 2 * HALF), stat,
            shape(256, 8 * HALF, BF16), shape(192, 4 * HALF, BF16),
        ],
        scal,
        act_a, act_b, stats_b, wsecond, wdown,
    )
    got_a, got_b = swap(edge, edge)
    stats_c = sum_parts(stats_c)
    merged, wide_c, stats_d, kept_c, kept_up = run(
        "stage_d",
        functools.partial(stage_d, members_c),
        [
            shape(128, 14 * HALF), shape(128, 8 * HALF), stat,
            shape(384, 4 * HALF, BF16), shape(384, 4 * HALF, BF16),
        ],
        scal,
        act_c, got_a, got_b, stats_c, wcoarse, wup, fine,
        scratch=[((128, 10 * HALF), F32)],
    )
    stats_d = sum_parts(stats_d)
    denoised, loss, back_d, edge_a, edge_b, stats_ed, grad_out = run(
        "stage_out",
        functools.partial(stage_out, members),
        [
            shape(96, 512), stat, shape(128, 8 * HALF),
            shape(128, 3 * HALF, BF16), shape(128, 3 * HALF, BF16), stat,
            shape(48, 192, BF16),
        ],
        scal,
        merged, stats_d, wout, wout_t, target, noise, line_a, line_b,
        scratch=[
            ((160, 512), F32), ((160, 512), F32), ((96, 8 * HALF), BF16), ((256, 8 * HALF), BF16),
            ((4, 96, 128), F32), ((4, 96, 128), F32), ((4, 96, 128), F32),
        ],
    )
    got_a, got_b = swap(edge_a, edge_b)
    stats_ed = sum_parts(stats_ed)
    grad_merged, back_c, grad_coarse, edge_a, edge_b, stats_ec, grad_up, grad_c = run(
        "stage_up",
        functools.partial(stage_up, members, members_c),
        [
            shape(128, 12 * HALF), shape(128, 4 * HALF), shape(128, 6 * HALF),
            shape(128, 3 * HALF, BF16), shape(128, 3 * HALF, BF16), stat,
            shape(192, 384, BF16), shape(384, 384, BF16),
        ],
        scal,
        merged, stats_d, stats_ed, back_d, got_a, got_b, kept_up, wup_t,
        wide_c, stats_c, kept_c, wcoarse_t,
        scratch=[
            ((384, 8 * HALF), BF16), ((384, 8 * HALF), BF16), ((384, 4 * HALF), BF16)
        ],
    )
    got_a, got_b = swap(edge_a, edge_b)
    stats_ec = sum_parts(stats_ec)
    grad_fine, back_b, stats_eb, grad_down, grad_second = run(
        "stage_down",
        functools.partial(stage_down, members, members_c),
        [
            shape(128, 8 * HALF), shape(128, 10 * HALF), stat,
            shape(384, 192, BF16), shape(192, 192, BF16),
        ],
        scal,
        stats_c, stats_ec, wide_c, back_c, grad_coarse, got_a, got_b,
        wdown_t, kept_pool, grad_merged, act_b, stats_b, kept_b, wsecond_t,
        scratch=[((384, 8 * HALF), BF16), ((384, 4 * HALF), BF16)],
    )
    stats_eb = sum_parts(stats_eb)
    back_a, stats_ea, grad_first, cell_sums = run(
        "stage_first",
        functools.partial(stage_first, members),
        [shape(128, 8 * HALF), stat, shape(192, 192, BF16), stat],
        scal,
        stats_b, stats_eb, act_b, back_b, wfirst_t, act_a, stats_a, kept_a,
        scratch=[((384, 8 * HALF), BF16)],
    )
    stats_ea = sum_parts(stats_ea)
    (grad_in,) = run(
        "stage_last",
        functools.partial(stage_last, members),
        [shape(192, 96, BF16)],
        None,
        stats_a, stats_ea, act_a, back_a, grad_fine, kept_in,
        scratch=[((128, 8 * HALF), BF16)],
    )

    loss_value = lax.psum(loss[0, 0], ("fsdp", "rows")) / members_all
    sums = cell_sums[0, :64] + cell_sums[0, 64:]
    embed_grad = (embedded.astype(F32)[:, None] * sums[None, :]).astype(BF16)

    def split(item, outs, ins, dim):
        width = item.shape[1] // 3
        taps = item.reshape(3, item.shape[0] // 3, 3, width)[:, :outs, :, :ins]
        taps = jnp.transpose(taps, (0, 2, 1, 3)).reshape(9, outs, ins)
        if dim == 1:
            parts = taps.reshape(9, count, outs // count, ins)
            return jnp.moveaxis(parts, 1, 0).reshape(count, -1)
        parts = taps.reshape(9, outs, count, ins // count)
        return jnp.moveaxis(parts, 2, 0).reshape(count, -1)

    done = reduce_gradients(
        [
            split(grad_in, 64, 24, 1),
            split(grad_first, 64, 64, 1),
            split(grad_second, 64, 64, 1),
            split(grad_down, 128, 64, 1),
            split(grad_c, 128, 128, 1),
            split(grad_up, 64, 128, 1),
            split(grad_out, 12, 64, 2),
            embed_grad.reshape(count, -1),
        ]
    )
    kernels = (
        input_kernel, first_kernel, second_kernel, down_kernel,
        coarse_kernel, upward_kernel, output_kernel, embed_matrix,
    )
    shards = [item.astype(F32).reshape(like.shape) for item, like in zip(done, kernels)]
    return (denoised.reshape(residual_target.shape), loss_value, *shards)


def solution(mesh):
    in_specs = (
        P("fsdp", None, "rows", None),
        P("fsdp", None, "rows", None),
        P("fsdp", None, "rows", None),
        P("fsdp"),
        P(None, "fsdp", None),
        P(None, "fsdp", None),
        P(None, "fsdp", None),
        P(None, "fsdp", None),
        P(None, "fsdp", None),
        P(None, "fsdp", None),
        P(None, None, "fsdp"),
        P("fsdp", None),
    )
    out_specs = (
        P("fsdp", None, "rows", None),
        P(),
        P(None, "fsdp", None),
        P(None, "fsdp", None),
        P(None, "fsdp", None),
        P(None, "fsdp", None),
        P(None, "fsdp", None),
        P(None, "fsdp", None),
        P(None, None, "fsdp"),
        P("fsdp", None),
    )
    return jax.shard_map(
        per_device, mesh=mesh, in_specs=in_specs, out_specs=out_specs, check_vma=False
    )
```

time: 824 us -> 273 us (0.33); the launches traced: 814 us -> 271 us
  blocking collectives: 338 us -> 92 us
  waiting for transfers between devices: 202 us -> 28.2 us
  matrix products: 92.8 us -> 0 us
  Pallas kernels: 0 us -> 62.3 us
  other arithmetic: 54 us -> 12.6 us
  local copies, waits for them, and re-layouts: 57.7 us -> 33.8 us
  between operations: 20.1 us -> 4.29 us
  starting transfers between devices: 48.7 us -> 37.7 us
    psum x9 -> x1, blocking collectives: 289 us -> 40.3 us  [per_device(): loss_value = lax.psum(loss[0, 0], ('fsdp', 'rows')) / members_all]
    psum x2 -> x0, waiting for transfers between devices: 141 us -> none  [the longest x1 87.7 us: per_device(): lax.psum(gradients[3].astype(jnp.bfloat16), 'rows').astype(jnp.float32)]
    dot_general x181 -> x0, matrix products: 92.8 us -> none  [the longest x117 51.4 us: tap_products(): jnp.einsum('oc,chw->ohw', kernels[position], window, preferred_element_ty...]
    pallas_call x0 -> x12, Pallas kernels: none -> 62.3 us  [run(): pl.pallas_call(kernel, out_shape=tuple(outs), in_specs=specs, out_specs=t...]
    all_to_all x0 -> x3, blocking collectives: none -> 51.7 us  [the longest x2 26.8 us: sum_parts(): lax.all_to_all(jnp.broadcast_to(stats[None], (count,) + stats.shape), 'ro...]
    all_gather x8 -> x0, blocking collectives: 49.5 us -> none  [the longest x1 9.7 us: per_device(): lax.all_gather(down_kernel.astype(jnp.bfloat16), 'fsdp', axis=1, tiled=True)]
    ppermute x26 -> x12, starting transfers between devices: 48.3 us -> 6.76 us  [the longest x5 3.34 us: swap(): lax.ppermute(value_b, 'rows', across)]
    reduce_scatter x5 -> x0, waiting for transfers between devices: 41.4 us -> none  [the longest x1 14.9 us: per_device(): lax.psum_scatter(band_sums[4].astype(jnp.bfloat16), 'fsdp', scatter_dimen...]
  transfers between devices with their start and end apart: 36 -> 19, of which waited for: 13 -> 8; matrix products, arithmetic and copies ran while one was open for 19% -> 8% of each run, Pallas kernels for 0% -> 4%
where the time goes in v1:
time: 273 us; the launch traced here: 271 us
  blocking collectives  92 us (34%)
  Pallas kernels  62.3 us (23%)
  starting transfers between devices  37.7 us (14%)
  local copies, waits for them, and re-layouts  33.8 us (12%)
  waiting for transfers between devices  28.2 us (10%)
  other arithmetic  12.6 us (5%)
  between operations  4.29 us (2%)
    pallas_call x12, Pallas kernels, run(): pl.pallas_call(kernel, out_shape=tuple(outs), in_specs=specs, out_specs=t...  62.3 us
    psum x1, blocking collectives, per_device(): loss_value = lax.psum(loss[0, 0], ('fsdp', 'rows')) / members_all  40.3 us
    all_to_all x6, waiting for transfers between devices, sum_parts(): lax.all_to_all(jnp.broadcast_to(stats[None], (count,) + stats.shape), 'ro...  27.5 us
    all_to_all x6, starting transfers between devices, sum_parts(): lax.all_to_all(jnp.broadcast_to(stats[None], (count,) + stats.shape), 'ro...  27.4 us
    all_to_all x2, blocking collectives, sum_parts(): lax.all_to_all(jnp.broadcast_to(stats[None], (count,) + stats.shape), 'ro...  26.8 us
    all_to_all x1, blocking collectives, reduce_gradients(): got = lax.all_to_all(flat, ('fsdp', 'rows'), 0, 0)  24.9 us
    broadcast_in_dim x8, local copies, waits for them, and re-layouts, sum_parts(): jnp.broadcast_to(stats[None], (count,) + stats.shape)  9.35 us
    unnamed x68, local copies, waits for them, and re-layouts  8.74 us
  transfers between devices with their start and end apart: 19, of which 8 were waited for; matrix products, arithmetic and copies ran while one was open for 8% of the time, Pallas kernels for 4%

profile of v1, /device:TPU:0, one launch (start us, length us, event | category | flops | bytes accessed | tf_op | source)
XLA Modules:
  0.0 270.9 jit_solution(17358680178549917667)
XLA Ops:
  2.3 2.4 enter.1
  10.0 2.5 collective-permute-start.2
  18.1 2.3 prepare_first.1
  21.2 4.3 %stage_a.1 = (f32[128,5120]{1,0:T(8,128)}, f32[8,128]{1,0:T(8,128)}, bf16[128,2560]{1,0:T(8,128)(2,1)}) custom-call(f32[9]{0:T(128)} %stack.44.scal, bf16[32,4096]{1,0:T(8,128)(2,1)} %get-tuple-element.70.own, bf16[32,3584]{1,0:T(8,128)(2,1)} %copy-done.11, bf16[32,3584]{1,0:T(8,128)(2,1)} %copy-done.12, bf16[384,128]{1,0:T(8,128)(2,1)} %get-tuple-element.73.win), custom_call_target="tpu_custom_call" | custom-call | tf_op jit(solution)/shard_map/stage_a/pallas_call | solution.py:707
  26.8 8.6 %all-to-all-start = ((f32[16,8,128]{2,1,0:T(8,128)}), f32[16,8,128]{2,1,0:T(8,128)S(1)}, u32[]{:S(2)}, u32[]{:S(2)}) async-start(f32[16,8,128]{2,1,0:T(8,128)} %broadcast_in_dim.21), calls=%async_computation | async-start | bytes 131072 | tf_op jit(solution)/shard_map/all_to_all | solution.py:720
  38.3 4.0 %all-to-all-done.stats_a = f32[16,8,128]{2,1,0:T(8,128)S(1)} async-done(((f32[16,8,128]{2,1,0:T(8,128)}), f32[16,8,128]{2,1,0:T(8,128)S(1)}, u32[]{:S(2)}, u32[]{:S(2)}) %all-to-all-start) | async-done | bytes 65568 | tf_op jit(solution)/shard_map/all_to_all | solution.py:720
  42.9 5.6 %stage_b.1 = (f32[128,4608]{1,0:T(8,128)}, f32[8,128]{1,0:T(8,128)}, bf16[256,2048]{1,0:T(8,128)(2,1)}) custom-call(f32[9]{0:T(128)} %stack.44.scal, f32[128,5120]{1,0:T(8,128)} %get-tuple-element.74.act_a, f32[16,8,128]{2,1,0:T(8,128)} %copy-done.1, bf16[384,256]{1,0:T(8,128)(2,1)} %get-tuple-element.76.wfirst, f32[128,128]{1,0:T(8,128)} %get-tuple-element.77.shift), custom_call_target="tpu_custom_call" | custom-call | tf_op jit(solution)/shard_map/stage_b/pallas_call | solution.py:707
  49.9 3.5 %all-to-all-start.1 = ((f32[16,8,128]{2,1,0:T(8,128)}), f32[16,8,128]{2,1,0:T(8,128)S(1)}, u32[]{:S(2)}, u32[]{:S(2)}) async-start(f32[16,8,128]{2,1,0:T(8,128)} %broadcast_in_dim.22), calls=%async_computation.1 | async-start | bytes 131072 | tf_op jit(solution)/shard_map/all_to_all | solution.py:720
  54.9 3.4 %prepare_rest.1 = (bf16[384,256]{1,0:T(8,128)(2,1)}, bf16[256,384]{1,0:T(8,128)(2,1)}, bf16[384,192]{1,0:T(8,128)(2,1)}, bf16[192,384]{1,0:T(8,128)(2,1)}, bf16[...) custom-call(bf16[576,64]{1,0:T(8,128)(2,1)} %bitcast.100, ...), custom_call_target="tpu_custom_call" | custom-call | tf_op jit(solution)/shard_map/prepare_rest/pallas_call | solution.py:707
  58.3 2.0 all-to-all-done.1.stats_b
  60.9 6.8 %stage_c.1 = (f32[128,4096]{1,0:T(8,128)}, f32[128,1536]{1,0:T(8,128)}, f32[128,512]{1,0:T(8,128)}, f32[8,128]{1,0:T(8,128)}, bf16[256,2048]{1,0:T(8,128)(2,1)}, /*index=5*/bf16[192,1024]{1,0:T(8,128)(2,1)}) custom-call(f32[9]{0:T(128)} %stack.44.scal, f32[128,5120]{1,0:T(8,128)} %get-tuple-element.74.act_a, f32[128,4608]{1,0:T(8,128)} %get-tuple-element.78.act_b, ...), custom_call_target="tpu_custom_call" | custom-call | tf_op jit(solution)/shard_map/stage_c/pallas_call | solution.py:707
  69.1 12.7 %all_to_all.50.stats_c = f32[16,8,128]{2,1,0:T(8,128)} all-to-all(f32[16,8,128]{2,1,0:T(8,128)S(1)} %broadcast_in_dim.23), channel_id=1, replica_groups=mesh['fsdp'=2,'rows'=16] {'rows'}, dimensions={0} | all-to-all | bytes 131072 | tf_op jit(solution)/shard_map/all_to_all | solution.py:720
  82.6 6.5 %stage_d.1 = (f32[128,3584]{1,0:T(8,128)}, f32[128,2048]{1,0:T(8,128)}, f32[8,128]{1,0:T(8,128)}, bf16[384,1024]{1,0:T(8,128)(2,1)}, bf16[384,1024]{1,0:T(8,128)(2,1)}) custom-call(f32[9]{0:T(128)} %stack.44.scal, f32[128,1536]{1,0:T(8,128)} %get-tuple-element.82.act_c, f32[128,512]{1,0:T(8,128)} %copy-done.9, f32[128,512]{1,0:T(8,128)} %copy-done.10, ...), custom_call_target="tpu_custom_call" | custom-call | tf_op jit(solution)/shard_map/stage_d/pallas_call | solution.py:707
  90.4 3.5 %all-to-all-start.3 = ((f32[16,8,128]{2,1,0:T(8,128)}), f32[16,8,128]{2,1,0:T(8,128)S(1)}, u32[]{:S(2)}, u32[]{:S(2)}) async-start(f32[16,8,128]{2,1,0:T(8,128)} %broadcast_in_dim.24), calls=%async_computation.3 | async-start | bytes 131072 | tf_op jit(solution)/shard_map/all_to_all | solution.py:720
  95.2 5.6 %all-to-all-done.3.stats_d = f32[16,8,128]{2,1,0:T(8,128)S(1)} async-done(((f32[16,8,128]{2,1,0:T(8,128)}), f32[16,8,128]{2,1,0:T(8,128)S(1)}, u32[]{:S(2)}, u32[]{:S(2)}) %all-to-all-start.3) | async-done | bytes 65568 | tf_op jit(solution)/shard_map/all_to_all | solution.py:720
  101.4 5.3 %stage_out.1 = (f32[96,512]{1,0:T(8,128)}, f32[8,128]{1,0:T(8,128)}, f32[128,2048]{1,0:T(8,128)}, bf16[128,768]{1,0:T(8,128)(2,1)}, bf16[128,768]{1,0:T(8,128)(2...) custom-call(f32[9]{0:T(128)} %stack.44.scal, f32[128,3584]{1,0:T(8,128)} %get-tuple-element.88.merged, ...), custom_call_target="tpu_custom_call" | custom-call | tf_op jit(solution)/shard_map/stage_out/pallas_call | solution.py:707
  108.1 14.1 %all_to_all.51.stats_ed = f32[16,8,128]{2,1,0:T(8,128)} all-to-all(f32[16,8,128]{2,1,0:T(8,128)S(1)} %broadcast_in_dim.25), channel_id=1, replica_groups=mesh['fsdp'=2,'rows'=16] {'rows'}, dimensions={0} | all-to-all | bytes 131072 | tf_op jit(solution)/shard_map/all_to_all | solution.py:720
  123.0 8.1 %stage_up.1 = (f32[128,3072]{1,0:T(8,128)}, f32[128,1024]{1,0:T(8,128)}, f32[128,1536]{1,0:T(8,128)}, bf16[128,768]{1,0:T(8,128)(2,1)}, bf16[128,768]{1,0:T(8,12...) custom-call(f32[9]{0:T(128)} %stack.44.scal, ...), custom_call_target="tpu_custom_call" | custom-call | tf_op jit(solution)/shard_map/stage_up/pallas_call | solution.py:707
  131.8 1.3 broadcast_in_dim.26
  133.1 4.7 %all-to-all-start.5 = ((f32[16,8,128]{2,1,0:T(8,128)}), f32[16,8,128]{2,1,0:T(8,128)S(1)}, u32[]{:S(2)}, u32[]{:S(2)}) async-start(f32[16,8,128]{2,1,0:T(8,128)} %broadcast_in_dim.26), calls=%async_computation.5 | async-start | bytes 131072 | tf_op jit(solution)/shard_map/all_to_all | solution.py:720
  138.4 6.4 %all-to-all-done.5.stats_ec = f32[16,8,128]{2,1,0:T(8,128)S(1)} async-done(((f32[16,8,128]{2,1,0:T(8,128)}), f32[16,8,128]{2,1,0:T(8,128)S(1)}, u32[]{:S(2)}, u32[]{:S(2)}) %all-to-all-start.5) | async-done | bytes 65568 | tf_op jit(solution)/shard_map/all_to_all | solution.py:720
  145.5 6.9 %stage_down.1 = (f32[128,2048]{1,0:T(8,128)}, f32[128,2560]{1,0:T(8,128)}, f32[8,128]{1,0:T(8,128)}, bf16[384,192]{1,0:T(8,128)(2,1)}, bf16[192,192]{1,0:T(8,128)(2,1)}) custom-call(f32[9]{0:T(128)} %stack.44.scal, f32[16,8,128]{2,1,0:T(8,128)} %all_to_all.50.stats_c, f32[16,8,128]{2,1,0:T(8,128)} %copy-done.7, f32[128,2048]{1,0:T(8,128)} %get-tuple-element.102.act_c, ...), custom_call_target="tpu_custom_call" | custom-call | tf_op jit(solution)/shard_map/stage_down/pallas_call | solution.py:707
  152.5 1.4 broadcast_in_dim.27
  153.8 3.5 %all-to-all-start.6 = ((f32[16,8,128]{2,1,0:T(8,128)}), f32[16,8,128]{2,1,0:T(8,128)S(1)}, u32[]{:S(2)}, u32[]{:S(2)}) async-start(f32[16,8,128]{2,1,0:T(8,128)} %broadcast_in_dim.27), calls=%async_computation.6 | async-start | bytes 131072 | tf_op jit(solution)/shard_map/all_to_all | solution.py:720
  159.3 4.9 %all-to-all-done.6.stats_eb = f32[16,8,128]{2,1,0:T(8,128)S(1)} async-done(((f32[16,8,128]{2,1,0:T(8,128)}), f32[16,8,128]{2,1,0:T(8,128)S(1)}, u32[]{:S(2)}, u32[]{:S(2)}) %all-to-all-start.6) | async-done | bytes 65568 | tf_op jit(solution)/shard_map/all_to_all | solution.py:720
  164.8 6.1 %stage_first.1 = (f32[128,2048]{1,0:T(8,128)}, f32[8,128]{1,0:T(8,128)}, bf16[192,192]{1,0:T(8,128)(2,1)}, f32[8,128]{1,0:T(8,128)}) custom-call(f32[9]{0:T(128)} %stack.44.scal, f32[16,8,128]{2,1,0:T(8,128)} %copy-done, f32[16,8,128]{2,1,0:T(8,128)} %copy-done.6, f32[128,4608]{1,0:T(8,128)} %get-tuple-element.78.act_b, ...), custom_call_target="tpu_custom_call" | custom-call | tf_op jit(solution)/shard_map/stage_first/pallas_call | solution.py:707
  172.3 3.5 %all-to-all-start.7 = ((f32[16,8,128]{2,1,0:T(8,128)}), f32[16,8,128]{2,1,0:T(8,128)S(1)}, u32[]{:S(2)}, u32[]{:S(2)}) async-start(f32[16,8,128]{2,1,0:T(8,128)} %broadcast_in_dim.28), calls=%async_computation.7 | async-start | bytes 131072 | tf_op jit(solution)/shard_map/all_to_all | solution.py:720
  177.9 4.7 %all-to-all-done.7.stats_ea = f32[16,8,128]{2,1,0:T(8,128)S(1)} async-done(((f32[16,8,128]{2,1,0:T(8,128)}), f32[16,8,128]{2,1,0:T(8,128)S(1)}, u32[]{:S(2)}, u32[]{:S(2)}) %all-to-all-start.7) | async-done | bytes 65568 | tf_op jit(solution)/shard_map/all_to_all | solution.py:720
  183.3 4.5 %stage_last.1 = bf16[192,96]{1,0:T(8,128)(2,1)} custom-call(f32[16,8,128]{2,1,0:T(8,128)} %copy-done.1, f32[16,8,128]{2,1,0:T(8,128)} %copy-done.8, f32[128,5120]{1,0:T(8,128)} %get-tuple-element.74.act_a, f32[128,2048]{1,0:T(8,128)} %get-tuple-element.120.back_a, f32[128,2048]{1,0:T(8,128)} %get-tuple-element.121.grad_fine, ...), custom_call_target="tpu_custom_call" | custom-call | tf_op jit(solution)/shard_map/stage_last/pallas_call | solution.py:707
  191.8 24.9 %all_to_all.52 = bf16[32,104,128]{2,1,0:T(8,128)(2,1)S(1)} all-to-all(bf16[32,104,128]{2,1,0:T(8,128)(2,1)S(1)} %reshape.331), channel_id=1, replica_groups=mesh['fsdp'=2,'rows'=16] {'fsdp','rows'}, dimensions={0} | all-to-all | bytes 1703936 | tf_op jit(solution)/shard_map/all_to_all | solution.py:759
  217.6 3.6 %all-to-all-start.9 = ((bf16[16,104,128]{2,1,0:T(8,128)(2,1)}), bf16[16,104,128]{2,1,0:T(8,128)(2,1)S(1)}, u32[]{:S(2)}, u32[]{:S(2)}) async-start(bf16[16,104,128]{2,1,0:T(8,128)(2,1)} %broadcast_in_dim.29), calls=%async_computation.9 | async-start | bytes 851968 | tf_op jit(solution)/shard_map/all_to_all | solution.py:761
  222.4 40.3 %psum.7 = f32[]{:T(128)} all-reduce(f32[]{:T(128)} %bitcast.21), channel_id=1, replica_groups=mesh['fsdp'=2,'rows'=16] {'fsdp','rows'}, use_global_device_ids=true, to_apply=%region_0.1 | all-reduce | flops 1 | bytes 8 | tf_op jit(solution)/shard_map/psum | solution.py:967
  (216 shorter events, 48.7 us)
Async XLA Ops:
  0.6 12.9 %copy-start.3 = (f32[9,64,64]{2,1,0:T(8,128)S(1)}, f32[9,64,64]{2,1,0:T(8,128)}, u32[]{:S(2)}) copy-start(f32[9,64,64]{2,1,0:T(8,128)} %param.19) | copy-start | bytes 442372
  0.7 13.1 %copy-start.4 = (f32[9,64,128]{2,1,0:T(8,128)S(1)}, f32[9,64,128]{2,1,0:T(8,128)}, u32[]{:S(2)}) copy-start(f32[9,64,128]{2,1,0:T(8,128)} %param.20) | copy-start | bytes 884740
  0.7 13.1 %copy-start.18 = (f32[9,32,128]{2,1,0:T(8,128)S(1)}, f32[9,32,128]{2,1,0:T(8,128)}, u32[]{:S(2)}) copy-start(f32[9,32,128]{2,1,0:T(8,128)} %param.21) | copy-start | bytes 442372
  0.7 13.1 %copy-start.21 = (f32[9,12,32]{2,1,0:T(8,128)S(1)}, f32[9,12,32]{2,1,0:T(8,128)}, u32[]{:S(2)}) copy-start(f32[9,12,32]{2,1,0:T(8,128)} %param.22) | copy-start | bytes 41476
  4.6 15.8 %collective-permute-start = (bf16[32,3584]{1,0:T(8,128)(2,1)}, bf16[32,3584]{1,0:T(8,128)(2,1)S(1)}, u32[]{:S(2)}, u32[]{:S(2)}) collective-permute-start(bf16[32,3584]{1,0:T(8,128)(2,1)} %get-tuple-element.71), channel_id=1, source_target_pairs={{0,1},{1,0},{2,3},{3,2},{4,5},{5,4},{6,7},{7,6},{8,9},{9,8},{10,11... | collective-permute-start | bytes 688136 | tf_op jit(solution)/shard_map/ppermute | solution.py:729
  5.1 15.3 %collective-permute-start.1 = (bf16[32,3584]{1,0:T(8,128)(2,1)}, bf16[32,3584]{1,0:T(8,128)(2,1)S(1)}, u32[]{:S(2)}, u32[]{:S(2)}) collective-permute-start(bf16[32,3584]{1,0:T(8,128)(2,1)} %get-tuple-element.72), channel_id=1, source_target_pairs={{1,2},{2,1},{3,4},{4,3},{5,6},{6,5},{7,8},{8,7},{9,10},{10,9},{11,... | collective-permute-start | bytes 688136 | tf_op jit(solution)/shard_map/ppermute | solution.py:729
  10.0 4.7 %collective-permute-start.2 = (bf16[29440]{0:T(1024)(128)(2,1)S(1)}, bf16[29440]{0:T(1024)(128)(2,1)S(1)}, u32[]{:S(2)}, u32[]{:S(2)}) collective-permute-start(bf16[29440]{0:T(1024)(128)(2,1)S(1)} %dynamic-update-slice.15), channel_id=1, source_target_pairs={{0,16},{16,0},{1,17},{17,1},{2,18},{18,2},{3,19},{19,3},{4,20},{20... | collective-permute-start | bytes 176648 | tf_op jit(solution)/shard_map/ppermute | solution.py:736
  14.0 21.4 %collective-permute-start.3 = (bf16[169344]{0:T(1024)(128)(2,1)S(1)}, bf16[169344]{0:T(1024)(128)(2,1)S(1)}, u32[]{:S(2)}, u32[]{:S(2)}) collective-permute-start(bf16[169344]{0:T(1024)(128)(2,1)S(1)} %constant_dynamic-update-slice_fusion.7), channel_id=1, source_target_pairs={{0,16},{16,0},{1,17},{17,1},{2,18},{18,2},{3,19},{19,3},{4,20},{20... | collective-permute-start | bytes 1016072 | tf_op jit(solution)/shard_map/ppermute | solution.py:736
  26.8 15.5 %all-to-all-start = ((f32[16,8,128]{2,1,0:T(8,128)}), f32[16,8,128]{2,1,0:T(8,128)S(1)}, u32[]{:S(2)}, u32[]{:S(2)}) async-start(f32[16,8,128]{2,1,0:T(8,128)} %broadcast_in_dim.21), calls=%async_computation | async-start | bytes 131072 | tf_op jit(solution)/shard_map/all_to_all | solution.py:720
  49.9 10.4 %all-to-all-start.1 = ((f32[16,8,128]{2,1,0:T(8,128)}), f32[16,8,128]{2,1,0:T(8,128)S(1)}, u32[]{:S(2)}, u32[]{:S(2)}) async-start(f32[16,8,128]{2,1,0:T(8,128)} %broadcast_in_dim.22), calls=%async_computation.1 | async-start | bytes 131072 | tf_op jit(solution)/shard_map/all_to_all | solution.py:720
  67.7 14.1 %collective-permute-start.4 = (f32[128,512]{1,0:T(8,128)}, f32[128,512]{1,0:T(8,128)S(1)}, u32[]{:S(2)}, u32[]{:S(2)}) collective-permute-start(f32[128,512]{1,0:T(8,128)} %get-tuple-element.83), channel_id=1, source_target_pairs={{0,1},{1,0},{2,3},{3,2},{4,5},{5,4},{6,7},{7,6},{8,9},{9,8},{10,11... | collective-permute-start | bytes 786440 | tf_op jit(solution)/shard_map/ppermute | solution.py:729
  67.7 14.1 %collective-permute-start.5 = (f32[128,512]{1,0:T(8,128)}, f32[128,512]{1,0:T(8,128)S(1)}, u32[]{:S(2)}, u32[]{:S(2)}) collective-permute-start(f32[128,512]{1,0:T(8,128)} %get-tuple-element.83), channel_id=1, source_target_pairs={{1,2},{2,1},{3,4},{4,3},{5,6},{6,5},{7,8},{8,7},{9,10},{10,9},{11,... | collective-permute-start | bytes 786440 | tf_op jit(solution)/shard_map/ppermute | solution.py:729
  82.6 11.3 %copy-start.26 = (f32[16,512]{1,0:T(8,128)S(1)}, f32[16,512]{1,0:T(8,128)}, u32[]{:S(2)}) copy-start(f32[16,512]{1,0:T(8,128)} %get-tuple-element.92) | copy-start | bytes 98308
  82.6 11.7 %copy-start.25 = (f32[16,512]{1,0:T(8,128)S(1)}, f32[16,512]{1,0:T(8,128)}, u32[]{:S(2)}) copy-start(f32[16,512]{1,0:T(8,128)} %get-tuple-element.93) | copy-start | bytes 98308
  90.4 10.4 %all-to-all-start.3 = ((f32[16,8,128]{2,1,0:T(8,128)}), f32[16,8,128]{2,1,0:T(8,128)S(1)}, u32[]{:S(2)}, u32[]{:S(2)}) async-start(f32[16,8,128]{2,1,0:T(8,128)} %broadcast_in_dim.24), calls=%async_computation.3 | async-start | bytes 131072 | tf_op jit(solution)/shard_map/all_to_all | solution.py:720
  93.9 1.3 collective-permute-start.6
  94.2 0.9 collective-permute-start.7
  95.2 5.6 %copy-start.22 = (f32[16,512]{1,0:T(8,128)}, f32[16,512]{1,0:T(8,128)S(1)}, u32[]{:S(2)}) copy-start(f32[16,512]{1,0:T(8,128)S(1)} %collective-permute-done.6.line_a) | copy-start | bytes 98308
  95.2 5.6 %copy-start.23 = (f32[16,512]{1,0:T(8,128)}, f32[16,512]{1,0:T(8,128)S(1)}, u32[]{:S(2)}) copy-start(f32[16,512]{1,0:T(8,128)S(1)} %collective-permute-done.7.line_b) | copy-start | bytes 98308
  106.7 15.5 %collective-permute-start.8 = (bf16[128,768]{1,0:T(8,128)(2,1)}, bf16[128,768]{1,0:T(8,128)(2,1)S(1)}, u32[]{:S(2)}, u32[]{:S(2)}) collective-permute-start(bf16[128,768]{1,0:T(8,128)(2,1)} %get-tuple-element.98), channel_id=1, source_target_pairs={{0,1},{1,0},{2,3},{3,2},{4,5},{5,4},{6,7},{7,6},{8,9},{9,8},{10,11... | collective-permute-start | bytes 589832 | tf_op jit(solution)/shard_map/ppermute | solution.py:729
  106.7 15.5 %collective-permute-start.9 = (bf16[128,768]{1,0:T(8,128)(2,1)}, bf16[128,768]{1,0:T(8,128)(2,1)S(1)}, u32[]{:S(2)}, u32[]{:S(2)}) collective-permute-start(bf16[128,768]{1,0:T(8,128)(2,1)} %get-tuple-element.99), channel_id=1, source_target_pairs={{1,2},{2,1},{3,4},{4,3},{5,6},{6,5},{7,8},{8,7},{9,10},{10,9},{11,... | collective-permute-start | bytes 589832 | tf_op jit(solution)/shard_map/ppermute | solution.py:729
  123.0 15.3 %copy-start.24 = (bf16[48,192]{1,0:T(8,128)(2,1)S(1)}, bf16[48,192]{1,0:T(8,128)(2,1)}, u32[]{:S(2)}) copy-start(bf16[48,192]{1,0:T(8,128)(2,1)} %get-tuple-element.128) | copy-start | bytes 55300
  131.1 13.7 %collective-permute-start.10 = (bf16[128,768]{1,0:T(8,128)(2,1)}, bf16[128,768]{1,0:T(8,128)(2,1)S(1)}, u32[]{:S(2)}, u32[]{:S(2)}) collective-permute-start(bf16[128,768]{1,0:T(8,128)(2,1)} %get-tuple-element.108), channel_id=1, source_target_pairs={{0,1},{1,0},{2,3},{3,2},{4,5},{5,4},{6,7},{7,6},{8,9},{9,8},{10,11... | collective-permute-start | bytes 589832 | tf_op jit(solution)/shard_map/ppermute | solution.py:729
  131.1 13.7 %collective-permute-start.11 = (bf16[128,768]{1,0:T(8,128)(2,1)}, bf16[128,768]{1,0:T(8,128)(2,1)S(1)}, u32[]{:S(2)}, u32[]{:S(2)}) collective-permute-start(bf16[128,768]{1,0:T(8,128)(2,1)} %get-tuple-element.109), channel_id=1, source_target_pairs={{1,2},{2,1},{3,4},{4,3},{5,6},{6,5},{7,8},{8,7},{9,10},{10,9},{11,... | collective-permute-start | bytes 589832 | tf_op jit(solution)/shard_map/ppermute | solution.py:729
  133.1 11.6 %all-to-all-start.5 = ((f32[16,8,128]{2,1,0:T(8,128)}), f32[16,8,128]{2,1,0:T(8,128)S(1)}, u32[]{:S(2)}, u32[]{:S(2)}) async-start(f32[16,8,128]{2,1,0:T(8,128)} %broadcast_in_dim.26), calls=%async_computation.5 | async-start | bytes 131072 | tf_op jit(solution)/shard_map/all_to_all | solution.py:720
  145.5 12.1 %copy-start.5 = (bf16[384,384]{1,0:T(8,128)(2,1)S(1)}, bf16[384,384]{1,0:T(8,128)(2,1)}, u32[]{:S(2)}) copy-start(bf16[384,384]{1,0:T(8,128)(2,1)} %get-tuple-element.126) | copy-start | bytes 884740
  152.5 5.4 %copy-start.19 = (bf16[192,384]{1,0:T(8,128)(2,1)S(1)}, bf16[192,384]{1,0:T(8,128)(2,1)}, u32[]{:S(2)}) copy-start(bf16[192,384]{1,0:T(8,128)(2,1)} %get-tuple-element.127) | copy-start | bytes 442372
  152.5 5.5 %copy-start.20 = (bf16[192,192]{1,0:T(8,128)(2,1)S(1)}, bf16[192,192]{1,0:T(8,128)(2,1)}, u32[]{:S(2)}) copy-start(bf16[192,192]{1,0:T(8,128)(2,1)} %get-tuple-element.124) | copy-start | bytes 221188
  153.8 10.4 %all-to-all-start.6 = ((f32[16,8,128]{2,1,0:T(8,128)}), f32[16,8,128]{2,1,0:T(8,128)S(1)}, u32[]{:S(2)}, u32[]{:S(2)}) async-start(f32[16,8,128]{2,1,0:T(8,128)} %broadcast_in_dim.27), calls=%async_computation.6 | async-start | bytes 131072 | tf_op jit(solution)/shard_map/all_to_all | solution.py:720
  157.5 0.9 copy-start.15
  172.3 10.4 %all-to-all-start.7 = ((f32[16,8,128]{2,1,0:T(8,128)}), f32[16,8,128]{2,1,0:T(8,128)S(1)}, u32[]{:S(2)}, u32[]{:S(2)}) async-start(f32[16,8,128]{2,1,0:T(8,128)} %broadcast_in_dim.28), calls=%async_computation.7 | async-start | bytes 131072 | tf_op jit(solution)/shard_map/all_to_all | solution.py:720
  217.6 45.7 %all-to-all-start.9 = ((bf16[16,104,128]{2,1,0:T(8,128)(2,1)}), bf16[16,104,128]{2,1,0:T(8,128)(2,1)S(1)}, u32[]{:S(2)}, u32[]{:S(2)}) async-start(bf16[16,104,128]{2,1,0:T(8,128)(2,1)} %broadcast_in_dim.29), calls=%async_computation.9 | async-start | bytes 851968 | tf_op jit(solution)/shard_map/all_to_all | solution.py:761
  (14 other events, 9.6 us)
